TPU v7x, 512 devices: a whole 4x4x16 slice. The times are simulated.
512 devices in a mesh: sta: 64 (over z, x_hi, core), freq: 8 (over y, x_lo).
Axes of the slice: x: 4 (x_hi: 2, x_lo: 2; x = x_hi * 2 + x_lo), y: 4, z: 16, core: 2. Of those that a mesh axis runs over, the one named last changes fastest.
Arguments:
- spectra: bfloat16 [2, 4096, 2048], P(None, 'sta', 'freq'), may hold values from -6 to 6
- station_ok: int32 [4096], P('sta'), may hold values 0 or 1
- pair_mask: int32 [4096, 3, 64], P('sta', None, 'freq'), may hold values 0 or 1
Outputs:
- correlations: float32 [4096, 3, 64, 512], P('sta', None, 'freq')
All inputs are finite; a program needn't handle non-finite values. No bound on the sum of `station_ok` or of `pair_mask` on one device may be relied on, other than what follows from the above.
Results may differ from a plain program's by a relative error of at most 0.0054.
Values may be sent and summed in bfloat16 or wider, within the bound.
No kernel may reach another device: no remote copies, remote signals or barrier semaphores. Data moves between devices by JAX's collectives and lax.ppermute only.
A program may use at most 64 MiB of HBM per device.

v0:
```python
import math

import jax
import jax.numpy as jnp
from jax import lax
from jax.sharding import PartitionSpec as P

F = 2048
L = 512
H = 4
SHIFTS = 3


epsilon = 1e-06


def extended(x, sides, width):
    for axis, dim in sides:
        devices, length = (lax.axis_size(axis), x.shape[dim])
        up = [(i, (i + 1) % devices) for i in range(devices - 1)]
        down = [(j, i) for i, j in up]
        last = lax.slice_in_dim(x, length - width, length, axis=dim)
        first = lax.slice_in_dim(x, 0, width, axis=dim)
        before = lax.ppermute(last, axis, up)
        after = lax.ppermute(first, axis, down)
        x = jnp.concatenate([before, x, after], axis=dim)
    return x


def from_behind(x, axis, by):
    devices = lax.axis_size(axis)
    return lax.ppermute(x, axis, [(i, (i + by) % devices) for i in range(devices)])


def lag_table(count):
    bins = jnp.arange(F, dtype=jnp.int32)
    lag_index = jnp.arange(count, dtype=jnp.int32) - L // 2
    phases = bins[:, None] * lag_index[None, :] % (2 * F)
    angles = phases.astype(jnp.float32) * (math.pi / F)
    return jnp.concatenate([jnp.cos(angles), -jnp.sin(angles)], axis=0).astype(jnp.bfloat16)


def cross_lags(own_band, partner, table):
    stations = own_band.shape[1]
    partners = partner.shape[1]
    group_rows = math.gcd(stations, 32)
    groups = stations // group_rows
    part_real = partner[0].astype(jnp.float32)[None]
    part_imag = partner[1].astype(jnp.float32)[None]
    blocks = own_band.reshape(2, groups, group_rows, own_band.shape[2]).transpose(1, 0, 2, 3)

    def group_lags(block):
        own_real = block[0].astype(jnp.float32)[:, None, :]
        own_imag = block[1].astype(jnp.float32)[:, None, :]
        cross_real = own_real * part_real + own_imag * part_imag
        cross_imag = own_imag * part_real - own_real * part_imag
        crossed = jnp.concatenate([cross_real, cross_imag], axis=-1).astype(jnp.bfloat16)
        crossed = crossed.reshape(group_rows * partners, crossed.shape[-1])
        lagged = jnp.dot(crossed, table, preferred_element_type=jnp.float32)
        return lagged.reshape(group_rows, partners, table.shape[1])

    return lax.map(group_lags, blocks).reshape(stations, partners, table.shape[1])


def shards(spectra, station_ok, pair_mask):
    bins_dev = spectra.shape[2]
    values = spectra.astype(jnp.float32)
    weight = station_ok.astype(jnp.float32)[:, None]
    powers = values[0] * values[0] + values[1] * values[1]
    padded = extended(powers, (("freq", 1),), H)
    smooth = jnp.zeros_like(powers)
    for offset in range(2 * H + 1):
        smooth = smooth + padded[:, offset : offset + bins_dev]
    smooth = smooth / (2 * H + 1)
    band_total = lax.psum(jnp.sum(powers, axis=1), "freq")
    band_mean = band_total / F
    scales = weight / jnp.sqrt(smooth + 0.5 * band_mean[:, None] + epsilon)
    whitened = (values * scales[None]).astype(jnp.bfloat16)
    stations = spectra.shape[1]
    part_rows = stations // lax.axis_size("freq")
    first_row = lax.axis_index("freq") * part_rows
    table = lag_table(L)
    own_band = lax.all_gather(whitened, "freq", axis=2, tiled=True)
    source = lax.dynamic_slice_in_dim(own_band, first_row, part_rows, 1)
    results = []
    carried = source
    for offset in range(1, SHIFTS + 1):
        carried = from_behind(carried, "sta", -1)
        results.append(cross_lags(own_band, carried, table))
    stacked = jnp.stack(results, axis=1) * (1.0 / math.sqrt(F))
    return stacked * pair_mask.astype(jnp.float32)[..., None]


def solution(mesh):
    return jax.shard_map(
        shards,
        mesh=mesh,
        in_specs=(P(None, "sta", "freq"), P("sta"), P("sta", None, "freq")),
        out_specs=P("sta", None, "freq", None),
        check_vma=False,
    )
```

profile of v0, /device:TPU:1, one launch (start us, length us, event | category | flops | bytes accessed | tf_op | source)
XLA Modules:
  0.0 125.5 jit_solution(12040716156369616052)
XLA Ops:
  0.0 0.8 convert_element_type.120
  1.0 3.9 %collective-permute-start = (f32[64,4]{1,0:T(8,128)S(1)}, f32[64,4]{1,0:T(8,128)S(1)}, u32[]{:S(2)}, u32[]{:S(2)}) collective-permute-start(f32[64,4]{1,0:T(8,128)S(1)} %get-tuple-element.160), channel_id=1, source_target_pairs={{0,1},{1,2},{2,3},{3,4},{4,5},{5,6},{6,7},{8,9},{9,10},{10,11},{11... | collective-permute-start | bytes 3080 | tf_op jit(solution)/shard_map/ppermute | solution.py:24
  5.0 1.3 %collective-permute-start.1 = (f32[64,4]{1,0:T(8,128)S(1)}, f32[64,4]{1,0:T(8,128)S(1)}, u32[]{:S(2)}, u32[]{:S(2)}) collective-permute-start(f32[64,4]{1,0:T(8,128)S(1)} %get-tuple-element.161), channel_id=1, source_target_pairs={{1,0},{2,1},{3,2},{4,3},{5,4},{6,5},{7,6},{9,8},{10,9},{11,10},{12... | collective-permute-start | bytes 3080 | tf_op jit(solution)/shard_map/ppermute | solution.py:25
  6.3 17.4 %psum.7 = f32[64]{0:T(128)S(1)} all-reduce(f32[64]{0:T(128)S(1)} %get-tuple-element.152), channel_id=1, replica_groups=mesh['sta'=64,'freq'=8] {'freq'}, use_global_device_ids=true, to_apply=%region_1.0 | all-reduce | flops 64 | bytes 512 | tf_op jit(solution)/shard_map/psum | solution.py:75
  23.7 17.0 %cosine_convert_fusion = (bf16[2048,512]{1,0:T(8,128)(2,1)S(1)}, bf16[2048,512]{1,0:T(8,128)(2,1)S(1)}) fusion(s32[512]{0:T(512)S(1)} %iota_add_fusion), kind=kLoop, calls=%fused_computation.50 | loop fusion | flops 17825792 | bytes 4196352 | tf_op jit(solution)/shard_map/convert.12
  40.7 2.2 %pad_maximum_fusion = bf16[4096,512]{1,0:T(8,128)(2,1)} fusion(bf16[2048,512]{1,0:T(8,128)(2,1)S(1)} %get-tuple-element.163, bf16[2048,512]{1,0:T(8,128)(2,1)S(1)} %get-tuple-element.162), kind=kLoop, calls=%fused_computation.48 | loop fusion | flops 8388608 | bytes 8388608 | tf_op jit(solution)/shard_map/concatenate | solution.py:40
  43.3 24.0 %all_gather.3 = bf16[2,64,2048]{2,1,0:T(8,128)(2,1)S(1)} all-gather(bf16[2,64,256]{2,1,0:T(8,128)(2,1)S(1)} %multiply_convert_fusion), channel_id=1, replica_groups=mesh['sta'=64,'freq'=8] {'freq'}, dimensions={2}, use_global_device_ids=true | all-gather | bytes 589824 | tf_op jit(solution)/shard_map/all_gather | solution.py:83
  67.3 13.5 %collective-permute-start.2 = (bf16[2,8,2048]{2,1,0:T(8,128)(2,1)S(1)}, bf16[2,8,2048]{2,1,0:T(8,128)(2,1)S(1)}, u32[]{:S(2)}, u32[]{:S(2)}) collective-permute-start(bf16[2,8,2048]{2,1,0:T(8,128)(2,1)S(1)} %constant_dynamic-slice_fusion), channel_id=1, source_target_pairs={{0,504},{8,0},{16,8},{24,16},{32,24},{40,32},{48,40},{56,48},{64,5... | collective-permute-start | bytes 196616 | tf_op jit(solution)/shard_map/ppermute | solution.py:32
  81.0 3.2 %collective-permute-done.2 = bf16[2,8,2048]{2,1,0:T(8,128)(2,1)S(1)} collective-permute-done((bf16[2,8,2048]{2,1,0:T(8,128)(2,1)S(1)}, bf16[2,8,2048]{2,1,0:T(8,128)(2,1)S(1)}, u32[]{:S(2)}, u32[]{:S(2)}) %collective-permute-start.2) | collective-permute-done | bytes 65568 | tf_op jit(solution)/shard_map/ppermute | solution.py:32
  84.3 1.9 %collective-permute-start.3 = (bf16[2,8,2048]{2,1,0:T(8,128)(2,1)S(1)}, bf16[2,8,2048]{2,1,0:T(8,128)(2,1)S(1)}, u32[]{:S(2)}, u32[]{:S(2)}) collective-permute-start(bf16[2,8,2048]{2,1,0:T(8,128)(2,1)S(1)} %collective-permute-done.2), channel_id=1, source_target_pairs={{0,504},{8,0},{16,8},{24,16},{32,24},{40,32},{48,40},{56,48},{64,5... | collective-permute-start | bytes 196616 | tf_op jit(solution)/shard_map/ppermute | solution.py:32
  86.3 8.2 %while.30 = (s32[]{:T(128)}, f32[2,32,8,512]{3,2,1,0:T(8,128)S(1)}, bf16[2,2,32,2048]{3,2,1,0:T(8,128)(2,1)S(1)}, f32[1,8,2048]{2,1,0:T(8,128)S(1)}, f32[1,8,204...) while((s32[]{:T(128)}, f32[2,32,8,512]{3,2,1,0:T(8,128)S(1)}, ...), condition=%wide.region_3.4_spmd, body=%wide.region_2.3_spmd.sunk | while | flops 1082261504 | bytes 10354805 | solution.py:62
  86.4 0.5 add_convert_fusion.6
  86.9 3.5 %fusion.98 = f32[2,32,8,512]{3,2,1,0:T(8,128)S(1)} fusion(f32[2,32,8,512]{3,2,1,0:T(8,128)S(1)} %get-tuple-element.363, s32[]{:T(128)} %get-tuple-element.362, bf16[4096,512]{1,0:T(8,128)(2,1)} %get-tuple-element.376, bf16[32,8,2048]{2,1,0:T(8,128)(2,1)S(1)} %get-tuple-element.277, bf16[32,8,2048]{2,1,0:T(8,128)(2,1)S(1)} %get-tuple-element.278), kind=kOutput, calls=%fused_computation.8.clone.1 | convolution fusion | flops 1077936128 | bytes 6815748 | tf_op jit(solution)/shard_map/while/body/eval_jaxpr/dot_general | solution.py:59
  90.5 0.5 add_convert_fusion.6
  91.0 3.5 %fusion.98 = f32[2,32,8,512]{3,2,1,0:T(8,128)S(1)} fusion(f32[2,32,8,512]{3,2,1,0:T(8,128)S(1)} %get-tuple-element.363, s32[]{:T(128)} %get-tuple-element.362, bf16[4096,512]{1,0:T(8,128)(2,1)} %get-tuple-element.376, bf16[32,8,2048]{2,1,0:T(8,128)(2,1)S(1)} %get-tuple-element.277, bf16[32,8,2048]{2,1,0:T(8,128)(2,1)S(1)} %get-tuple-element.278), kind=kOutput, calls=%fused_computation.8.clone.1 | convolution fusion | flops 1077936128 | bytes 6815748 | tf_op jit(solution)/shard_map/while/body/eval_jaxpr/dot_general | solution.py:59
  94.5 10.3 %collective-permute-start.4 = (bf16[2,8,2048]{2,1,0:T(8,128)(2,1)S(1)}, bf16[2,8,2048]{2,1,0:T(8,128)(2,1)S(1)}, u32[]{:S(2)}, u32[]{:S(2)}) collective-permute-start(bf16[2,8,2048]{2,1,0:T(8,128)(2,1)S(1)} %collective-permute-done.3), channel_id=1, source_target_pairs={{0,504},{8,0},{16,8},{24,16},{32,24},{40,32},{48,40},{56,48},{64,5... | collective-permute-start | bytes 196616 | tf_op jit(solution)/shard_map/ppermute | solution.py:32
  104.9 8.2 %while.31 = (s32[]{:T(128)}, f32[2,32,8,512]{3,2,1,0:T(8,128)S(1)}, bf16[2,2,32,2048]{3,2,1,0:T(8,128)(2,1)S(1)}, f32[1,8,2048]{2,1,0:T(8,128)S(1)}, f32[1,8,204...) while((s32[]{:T(128)}, f32[2,32,8,512]{3,2,1,0:T(8,128)S(1)}, ...), condition=%wide.region_5.6_spmd, body=%wide.region_4.5_spmd.sunk | while | flops 1082261504 | bytes 10354805 | solution.py:62
  105.5 3.5 %fusion.102 = f32[2,32,8,512]{3,2,1,0:T(8,128)S(1)} fusion(f32[2,32,8,512]{3,2,1,0:T(8,128)S(1)} %get-tuple-element.336, s32[]{:T(128)} %get-tuple-element.335, bf16[4096,512]{1,0:T(8,128)(2,1)} %get-tuple-element.349, bf16[32,8,2048]{2,1,0:T(8,128)(2,1)S(1)} %get-tuple-element.287, bf16[32,8,2048]{2,1,0:T(8,128)(2,1)S(1)} %get-tuple-element.288), kind=kOutput, calls=%fused_computation.22.clone.1 | convolution fusion | flops 1077936128 | bytes 6815748 | tf_op jit(solution)/shard_map/while/body/eval_jaxpr/dot_general | solution.py:59
  109.6 3.5 %fusion.102 = f32[2,32,8,512]{3,2,1,0:T(8,128)S(1)} fusion(f32[2,32,8,512]{3,2,1,0:T(8,128)S(1)} %get-tuple-element.336, s32[]{:T(128)} %get-tuple-element.335, bf16[4096,512]{1,0:T(8,128)(2,1)} %get-tuple-element.349, bf16[32,8,2048]{2,1,0:T(8,128)(2,1)S(1)} %get-tuple-element.287, bf16[32,8,2048]{2,1,0:T(8,128)(2,1)S(1)} %get-tuple-element.288), kind=kOutput, calls=%fused_computation.22.clone.1 | convolution fusion | flops 1077936128 | bytes 6815748 | tf_op jit(solution)/shard_map/while/body/eval_jaxpr/dot_general | solution.py:59
  113.1 0.9 copy-done
  114.2 8.2 %while.32 = (s32[]{:T(128)}, f32[2,32,8,512]{3,2,1,0:T(8,128)S(1)}, bf16[2,2,32,2048]{3,2,1,0:T(8,128)(2,1)S(1)}, f32[1,8,2048]{2,1,0:T(8,128)S(1)}, f32[1,8,204...) while((s32[]{:T(128)}, f32[2,32,8,512]{3,2,1,0:T(8,128)S(1)}, ...), condition=%wide.region_7.8_spmd, body=%wide.region_6.7_spmd.sunk | while | flops 1082261504 | bytes 10354805 | solution.py:62
  114.8 3.5 %fusion.106 = f32[2,32,8,512]{3,2,1,0:T(8,128)S(1)} fusion(f32[2,32,8,512]{3,2,1,0:T(8,128)S(1)} %get-tuple-element.309, s32[]{:T(128)} %get-tuple-element.308, bf16[4096,512]{1,0:T(8,128)(2,1)} %get-tuple-element.322, bf16[32,8,2048]{2,1,0:T(8,128)(2,1)S(1)} %get-tuple-element.297, bf16[32,8,2048]{2,1,0:T(8,128)(2,1)S(1)} %get-tuple-element.298), kind=kOutput, calls=%fused_computation.36.clone.1 | convolution fusion | flops 1077936128 | bytes 6815748 | tf_op jit(solution)/shard_map/while/body/eval_jaxpr/dot_general | solution.py:59
  118.9 3.5 %fusion.106 = f32[2,32,8,512]{3,2,1,0:T(8,128)S(1)} fusion(f32[2,32,8,512]{3,2,1,0:T(8,128)S(1)} %get-tuple-element.309, s32[]{:T(128)} %get-tuple-element.308, bf16[4096,512]{1,0:T(8,128)(2,1)} %get-tuple-element.322, bf16[32,8,2048]{2,1,0:T(8,128)(2,1)S(1)} %get-tuple-element.297, bf16[32,8,2048]{2,1,0:T(8,128)(2,1)S(1)} %get-tuple-element.298), kind=kOutput, calls=%fused_computation.36.clone.1 | convolution fusion | flops 1077936128 | bytes 6815748 | tf_op jit(solution)/shard_map/while/body/eval_jaxpr/dot_general | solution.py:59
  122.3 3.2 %maximum_multiply_fusion = f32[64,3,8,512]{3,2,1,0:T(8,128)} fusion(f32[64,1,8,512]{3,2,1,0:T(8,128)S(1)} %bitcast.109, f32[64,1,8,512]{3,2,1,0:T(8,128)} %bitcast.111, f32[64,1,8,512]{3,2,1,0:T(8,128)S(1)} %bitcast.110, f32[64,3,8]{2,1,0:T(4,128)S(1)} %copy.5), kind=kLoop, calls=%fused_computation.54 | loop fusion | flops 2359296 | bytes 6297600 | tf_op jit(solution)/shard_map/mul | solution.py:91
  (38 shorter events, 3.5 us)
Async XLA Ops:
  1.0 41.9 %collective-permute-start = (f32[64,4]{1,0:T(8,128)S(1)}, f32[64,4]{1,0:T(8,128)S(1)}, u32[]{:S(2)}, u32[]{:S(2)}) collective-permute-start(f32[64,4]{1,0:T(8,128)S(1)} %get-tuple-element.160), channel_id=1, source_target_pairs={{0,1},{1,2},{2,3},{3,4},{4,5},{5,6},{6,7},{8,9},{9,10},{10,11},{11... | collective-permute-start | bytes 3080 | tf_op jit(solution)/shard_map/ppermute | solution.py:24
  5.0 38.0 %collective-permute-start.1 = (f32[64,4]{1,0:T(8,128)S(1)}, f32[64,4]{1,0:T(8,128)S(1)}, u32[]{:S(2)}, u32[]{:S(2)}) collective-permute-start(f32[64,4]{1,0:T(8,128)S(1)} %get-tuple-element.161), channel_id=1, source_target_pairs={{1,0},{2,1},{3,2},{4,3},{5,4},{6,5},{7,6},{9,8},{10,9},{11,10},{12... | collective-permute-start | bytes 3080 | tf_op jit(solution)/shard_map/ppermute | solution.py:25
  40.7 2.3 %copy-start.3 = (s32[64]{0:T(128)S(1)}, s32[64]{0:T(128)}, u32[]{:S(2)}) copy-start(s32[64]{0:T(128)} %param.10) | copy-start | bytes 772
  40.7 2.6 %copy-start.1 = (bf16[2,64,256]{2,1,0:T(8,128)(2,1)S(1)}, bf16[2,64,256]{2,1,0:T(8,128)(2,1)}, u32[]{:S(2)}) copy-start(bf16[2,64,256]{2,1,0:T(8,128)(2,1)} %param.9) | copy-start | bytes 196612
  40.7 40.1 %copy-start.2 = (s32[64,3,8]{0,2,1:T(8,128)S(1)}, s32[64,3,8]{0,2,1:T(8,128)}, u32[]{:S(2)}) copy-start(s32[64,3,8]{0,2,1:T(8,128)} %param.11) | copy-start | bytes 18436
  67.3 16.9 %collective-permute-start.2 = (bf16[2,8,2048]{2,1,0:T(8,128)(2,1)S(1)}, bf16[2,8,2048]{2,1,0:T(8,128)(2,1)S(1)}, u32[]{:S(2)}, u32[]{:S(2)}) collective-permute-start(bf16[2,8,2048]{2,1,0:T(8,128)(2,1)S(1)} %constant_dynamic-slice_fusion), channel_id=1, source_target_pairs={{0,504},{8,0},{16,8},{24,16},{32,24},{40,32},{48,40},{56,48},{64,5... | collective-permute-start | bytes 196616 | tf_op jit(solution)/shard_map/ppermute | solution.py:32
  84.3 10.2 %collective-permute-start.3 = (bf16[2,8,2048]{2,1,0:T(8,128)(2,1)S(1)}, bf16[2,8,2048]{2,1,0:T(8,128)(2,1)S(1)}, u32[]{:S(2)}, u32[]{:S(2)}) collective-permute-start(bf16[2,8,2048]{2,1,0:T(8,128)(2,1)S(1)} %collective-permute-done.2), channel_id=1, source_target_pairs={{0,504},{8,0},{16,8},{24,16},{32,24},{40,32},{48,40},{56,48},{64,5... | collective-permute-start | bytes 196616 | tf_op jit(solution)/shard_map/ppermute | solution.py:32
  94.5 18.6 %collective-permute-start.4 = (bf16[2,8,2048]{2,1,0:T(8,128)(2,1)S(1)}, bf16[2,8,2048]{2,1,0:T(8,128)(2,1)S(1)}, u32[]{:S(2)}, u32[]{:S(2)}) collective-permute-start(bf16[2,8,2048]{2,1,0:T(8,128)(2,1)S(1)} %collective-permute-done.3), channel_id=1, source_target_pairs={{0,504},{8,0},{16,8},{24,16},{32,24},{40,32},{48,40},{56,48},{64,5... | collective-permute-start | bytes 196616 | tf_op jit(solution)/shard_map/ppermute | solution.py:32
  113.1 1.0 copy-start
where the time goes:
time: 126 us
  blocking collectives  41.4 us (33%)
  starting transfers between devices  30.9 us (25%)
  other arithmetic  27.2 us (22%)
  matrix products  20.8 us (17%)
  waiting for transfers between devices  3.26 us (3%)
  local copies, waits for them, and re-layouts  1.53 us (1%)
    ppermute x3, starting transfers between devices, from_behind(): lax.ppermute(x, axis, [(i, (i + by) % devices) for i in range(devices)])  25.7 us
    all_gather x1, blocking collectives, shards(): own_band = lax.all_gather(whitened, 'freq', axis=2, tiled=True)  24 us
    dot_general x6, matrix products, group_lags(): lagged = jnp.dot(crossed, table, preferred_element_type=jnp.float32)  20.8 us
    another operation x7, other arithmetic  20.2 us
    psum x1, blocking collectives, shards(): band_total = lax.psum(jnp.sum(powers, axis=1), 'freq')  17.4 us
    ppermute x1, starting transfers between devices, extended(): before = lax.ppermute(last, axis, up)  3.95 us
    ppermute x3, waiting for transfers between devices, from_behind(): lax.ppermute(x, axis, [(i, (i + by) % devices) for i in range(devices)])  3.25 us
    mul x2, other arithmetic, shards(): return stacked * pair_mask.astype(jnp.float32)[..., None]  3.18 us
  transfers between devices with their start and end apart: 5, of which 1 were waited for; matrix products, arithmetic and copies ran while one was open for 29% of the time, Pallas kernels for 0%

commit v1 on v0

v1 whole, which is shorter than its diff:
```python
import math

import jax
import jax.numpy as jnp
import numpy as np
import ml_dtypes
from jax import lax
from jax.experimental import pallas as pl
from jax.experimental.pallas import tpu as pltpu
from jax.sharding import Mesh, PartitionSpec as P

F = 2048
L = 512
H = 4
SHIFTS = 3
HALF = L // 2
LAYER = 4
epsilon = 1e-06
MIB = 1024 * 1024


def tables():
    bins = np.arange(F, dtype=np.int64)
    taus = np.arange(HALF, dtype=np.int64)
    angles = (bins[:, None] * taus[None, :] % (2 * F)).astype(np.float64) * (math.pi / F)
    edge = (bins * HALF % (2 * F)).astype(np.float64) * (math.pi / F)
    bf16 = ml_dtypes.bfloat16
    last = np.stack([np.cos(edge), np.sin(edge)] * 4).astype(bf16).astype(np.float32)
    return np.cos(angles).astype(bf16), (-np.sin(angles)).astype(bf16), last


def whitened(real, imag):
    rows = real.shape[0]
    powers = real * real + imag * imag
    total = jnp.sum(powers, axis=1, keepdims=True)
    padded = jnp.concatenate([powers, jnp.zeros((rows, 128), jnp.float32)], axis=1)
    width = padded.shape[1]
    two = padded + pltpu.roll(padded, 1, 1)
    four = two + pltpu.roll(two, 2, 1)
    eight = four + pltpu.roll(four, 4, 1)
    nine = eight + pltpu.roll(padded, 2 * H, 1)
    smooth = pltpu.roll(nine, width - H, 1)[:, :F]
    scales = lax.rsqrt(smooth * (1.0 / (2 * H + 1)) + total * (0.5 / F) + epsilon)
    return real * scales, imag * scales


def prepare(spectra_hbm, ok_hbm, repeated_ref, source_ref, spectra_ref, ok_ref, valid_ref, turned_ref, sems):
    stations = spectra_ref.shape[1]
    bands, both_rows, _ = source_ref.shape
    partners = both_rows // 2
    loads = [pltpu.make_async_copy(spectra_hbm, spectra_ref, sems.at[0]), pltpu.make_async_copy(ok_hbm, ok_ref, sems.at[1])]
    for load in loads:
        load.start()
    for load in loads:
        load.wait()
    shape = (stations, stations)
    here = lax.broadcasted_iota(jnp.int32, shape, 0) == lax.broadcasted_iota(jnp.int32, shape, 1)
    ok = jnp.where(here, jnp.broadcast_to(ok_ref[...].astype(jnp.float32), shape), 0.0)
    ok = jnp.sum(ok, axis=1, keepdims=True)
    real = spectra_ref[0].astype(jnp.float32) * ok
    imag = spectra_ref[1].astype(jnp.float32) * ok
    valid_ref[0] = real.astype(jnp.bfloat16)
    valid_ref[1] = imag.astype(jnp.bfloat16)
    stores = [pltpu.make_async_copy(valid_ref, repeated_ref.at[q], sems.at[2 + q]) for q in range(bands)]
    for store in stores:
        store.start()
    for q in range(bands):
        rows = slice(q * partners, (q + 1) * partners)
        turned_ref[q] = jnp.concatenate([real[rows], imag[rows]], axis=0).astype(jnp.bfloat16)
    stores.append(pltpu.make_async_copy(turned_ref, source_ref, sems.at[2 + bands]))
    stores[-1].start()
    for store in stores:
        store.wait()


def prepared(spectra, station_ok, bands):
    _, stations, bins = spectra.shape
    turned = (bands, 2 * stations // bands, bins)
    hbm = pl.BlockSpec(memory_space=pl.ANY)
    return pl.pallas_call(
        prepare,
        out_shape=[jax.ShapeDtypeStruct((bands,) + spectra.shape, spectra.dtype),
                   jax.ShapeDtypeStruct(turned, spectra.dtype)],
        in_specs=[hbm] * 2,
        out_specs=[hbm] * 2,
        scratch_shapes=[
            pltpu.VMEM(spectra.shape, spectra.dtype),
            pltpu.VMEM((1, stations), jnp.int32),
            pltpu.VMEM(spectra.shape, spectra.dtype),
            pltpu.VMEM(turned, spectra.dtype),
            pltpu.SemaphoreType.DMA((3 + bands,)),
        ],
        compiler_params=pltpu.CompilerParams(vmem_limit_bytes=60 * MIB),
        cost_estimate=pl.CostEstimate(flops=spectra.size, bytes_accessed=2 * 10 * spectra.size, transcendentals=0),
    )(spectra, station_ok.reshape(1, stations))


def choose(place_ref, source_ref, above_ref, sent_ref):
    bands = source_ref.shape[0]
    for other in range(LAYER):
        to = sent_ref.at[other * bands:(other + 1) * bands]

        @pl.when(other < place_ref[0])
        def _():
            to[...] = source_ref[...]

        @pl.when(other >= place_ref[0])
        def _():
            to[...] = above_ref[...]


def chosen(place, source, above):
    vmem = pl.BlockSpec(memory_space=pltpu.VMEM)
    return pl.pallas_call(
        choose,
        out_shape=jax.ShapeDtypeStruct((LAYER * source.shape[0],) + source.shape[1:], source.dtype),
        in_specs=[pl.BlockSpec(memory_space=pltpu.SMEM)] + [vmem] * 2,
        out_specs=vmem,
        compiler_params=pltpu.CompilerParams(vmem_limit_bytes=8 * MIB),
        cost_estimate=pl.CostEstimate(flops=0, bytes_accessed=2 * 6 * source.size, transcendentals=0),
    )(place, source, above)


def whiten(own_ref, cos_from, sin_from, last_from, real_ref, imag_ref, cos_ref, sin_ref, last_ref, sems):
    bands = own_ref.shape[0]
    pairs = ((cos_from, cos_ref), (sin_from, sin_ref), (last_from, last_ref))
    loads = [pltpu.make_async_copy(table, to, sems.at[i]) for i, (table, to) in enumerate(pairs)]
    for load in loads:
        load.start()

    def some(group, carry):
        at = pl.ds(pl.multiple_of(group * 16, 16), 16)
        real = jnp.concatenate([own_ref[q, 0, at, :] for q in range(bands)], axis=1)
        imag = jnp.concatenate([own_ref[q, 1, at, :] for q in range(bands)], axis=1)
        real, imag = whitened(real.astype(jnp.float32), imag.astype(jnp.float32))
        real_ref[at, :] = real.astype(jnp.bfloat16)
        imag_ref[at, :] = imag.astype(jnp.bfloat16)
        return carry

    lax.fori_loop(0, real_ref.shape[0] // 16, some, 0)
    for load in loads:
        load.wait()


def whitened_block(own):
    stations = own.shape[2]
    given = [jnp.asarray(table) for table in tables()]
    vmem = pl.BlockSpec(memory_space=pltpu.VMEM)
    return pl.pallas_call(
        whiten,
        out_shape=[jax.ShapeDtypeStruct((stations, F), jnp.bfloat16)] * 2
        + [jax.ShapeDtypeStruct(table.shape, table.dtype) for table in given],
        in_specs=[vmem] + [pl.BlockSpec(memory_space=pl.ANY)] * 3,
        out_specs=[vmem] * 5,
        scratch_shapes=[pltpu.SemaphoreType.DMA((3,))],
        compiler_params=pltpu.CompilerParams(vmem_limit_bytes=8 * MIB),
        cost_estimate=pl.CostEstimate(flops=30 * stations * F, bytes_accessed=8 * stations * F, transcendentals=stations * F),
    )(own, *given)


def correlate(place_ref, own_real, own_imag, cos_ref, sin_ref, last_ref, part_ref, mask_ref, out_ref,
              part_real, part_imag, turned, cross_real, cross_imag, lags, sems):
    stations = own_real.shape[0]
    bands = part_ref.shape[0] // LAYER
    partners = part_ref.shape[1] // 2
    last_cos = last_ref[0:1, :]
    last_sin = last_ref[1:2, :]
    for k in range(SHIFTS):
        first = lax.rem(place_ref[0] + (k + 1), LAYER) * bands
        both = jnp.concatenate([part_ref[first + q] for q in range(bands)], axis=1).astype(jnp.float32)
        real, imag = whitened(both[:partners], both[partners:])
        real = real.astype(jnp.bfloat16).astype(jnp.float32)
        imag = imag.astype(jnp.bfloat16).astype(jnp.float32)
        part_real[k * partners:(k + 1) * partners, :] = real
        part_imag[k * partners:(k + 1) * partners, :] = imag
        turned[0, k * partners:(k + 1) * partners, :] = real * last_cos - imag * last_sin
        turned[1, k * partners:(k + 1) * partners, :] = imag * last_cos + real * last_sin

    edge = jnp.zeros((stations, SHIFTS * partners), jnp.float32)
    for c, own in ((0, own_real), (1, own_imag)):
        high = turned[c].astype(jnp.bfloat16)
        low = (turned[c] - high.astype(jnp.float32)).astype(jnp.bfloat16)
        for part in (high, low):
            edge = edge + lax.dot_general(own[...], part, (((1,), (1,)), ((), ())),
                                          preferred_element_type=jnp.float32)
    edge = edge * mask_ref[...]

    def finished(k, q):
        rows = lags.at[k, q].reshape(stations, partners, 128)
        return pltpu.make_async_copy(rows, out_ref.at[:, k, :, pl.ds(q * 128, 128)], sems.at[k, q])

    lane = lax.broadcasted_iota(jnp.int32, (stations, 128), 1)
    mirror = lax.rem(128 - lane, 128)
    for k in range(SHIFTS):
        def cross(j, carry):
            row = k * partners + j
            at = pl.ds(pl.multiple_of(j * stations, 16), stations)
            other_real = jnp.broadcast_to(part_real[pl.ds(row, 1), :], (16, F)).astype(jnp.bfloat16)
            other_imag = jnp.broadcast_to(part_imag[pl.ds(row, 1), :], (16, F)).astype(jnp.bfloat16)
            for g in range(stations // 16):
                real = own_real[g * 16:(g + 1) * 16, :]
                imag = own_imag[g * 16:(g + 1) * 16, :]
                at = pl.ds(pl.multiple_of(j * stations + g * 16, 16), 16)
                cross_real[at, :] = real * other_real + imag * other_imag
                cross_imag[at, :] = imag * other_real - real * other_imag
            return carry

        lax.fori_loop(0, partners, cross, 0)
        even = jnp.dot(cross_real[...], cos_ref[...], preferred_element_type=jnp.float32)
        odd = jnp.dot(cross_imag[...], sin_ref[...], preferred_element_type=jnp.float32)
        for j in range(partners):
            column = k * partners + j
            weight = mask_ref[:, column:column + 1]
            c = even[j * stations:(j + 1) * stations, :] * weight
            s = odd[j * stations:(j + 1) * stations, :] * weight
            up = c + s
            down = c - s
            near, far = down[:, :128], down[:, 128:]
            ends = jnp.broadcast_to(edge[:, column:column + 1], (stations, 128))
            first = jnp.take_along_axis(jnp.where(lane == 0, ends, far), mirror, axis=1)
            second = jnp.take_along_axis(jnp.where(lane == 0, far, near), mirror, axis=1)
            at = pl.ds(j, stations, stride=partners)
            for q, piece in enumerate((first, second, up[:, :128], up[:, 128:])):
                lags[k, q, at, :] = piece
        for q in range(4):
            finished(k, q).start()
    for k in range(SHIFTS):
        for q in range(4):
            finished(k, q).wait()


def correlations_of(place, own, parts, mask):
    stations = own[0].shape[0]
    partners = parts.shape[1] // 2
    vmem = pl.BlockSpec(memory_space=pltpu.VMEM)
    return pl.pallas_call(
        correlate,
        out_shape=jax.ShapeDtypeStruct((stations, SHIFTS, partners, L), jnp.float32),
        in_specs=[pl.BlockSpec(memory_space=pltpu.SMEM)] + [vmem] * 7,
        out_specs=pl.BlockSpec(memory_space=pl.ANY),
        scratch_shapes=[
            pltpu.VMEM((SHIFTS * partners, F), jnp.float32),
            pltpu.VMEM((SHIFTS * partners, F), jnp.float32),
            pltpu.VMEM((2, SHIFTS * partners, F), jnp.float32),
            pltpu.VMEM((stations * partners, F), jnp.bfloat16),
            pltpu.VMEM((stations * partners, F), jnp.bfloat16),
            pltpu.VMEM((SHIFTS, L // 128, stations * partners, 128), jnp.float32),
            pltpu.SemaphoreType.DMA((SHIFTS, L // 128)),
        ],
        compiler_params=pltpu.CompilerParams(vmem_limit_bytes=24 * MIB),
        cost_estimate=pl.CostEstimate(
            flops=2 * SHIFTS * stations * partners * 2 * F * HALF,
            bytes_accessed=SHIFTS * stations * partners * L * 4,
            transcendentals=0),
    )(place, *own, parts, mask)


def shards(spectra, station_ok, pair_mask):
    bands, layers = lax.axis_size("freq"), lax.axis_size("layer")
    stations = spectra.shape[1]
    partners = stations // bands
    repeated, source = prepared(spectra, station_ok, bands)
    own = lax.all_to_all(repeated, "freq", 0, 0)
    above = lax.ppermute(source, "layer", [((i + 1) % layers, i) for i in range(layers)])
    above, own = lax.optimization_barrier((above, own))
    place = lax.axis_index("block").reshape(1)
    parts = lax.all_to_all(chosen(place, source, above), ("block", "freq"), 0, 0)
    mask = pair_mask.reshape(stations, SHIFTS * partners).astype(jnp.float32) * (1.0 / math.sqrt(F))
    return correlations_of(place, whitened_block(own), parts, mask)


def solution(mesh):
    blocks, bands = mesh.shape["sta"], mesh.shape["freq"]
    inner = Mesh(mesh.devices.reshape(blocks // LAYER, LAYER, bands), ("layer", "block", "freq"))
    sta = ("layer", "block")
    return jax.shard_map(
        shards,
        mesh=inner,
        in_specs=(P(None, sta, "freq"), P(sta), P(sta, None, "freq")),
        out_specs=P(sta, None, "freq", None),
        check_vma=False,
    )
```

time: 126 us -> 48.9 us (0.39)
  blocking collectives: 41.4 us -> 0 us
  other arithmetic: 27.2 us -> 0.71 us
  matrix products: 20.8 us -> 0 us
  Pallas kernels: 0 us -> 13 us
  starting transfers between devices: 30.9 us -> 26 us
  local copies, waits for them, and re-layouts: 1.53 us -> 4.21 us
    all_gather x1 -> x0, blocking collectives: 24 us -> none  [shards(): own_band = lax.all_gather(whitened, 'freq', axis=2, tiled=True)]
    dot_general x6 -> x0, matrix products: 20.8 us -> none  [group_lags(): lagged = jnp.dot(crossed, table, preferred_element_type=jnp.float32)]
    another operation x7 -> x0, other arithmetic: 20.2 us -> none
    ppermute x5 -> x1, starting transfers between devices: 30.9 us -> 11.1 us  [shards(): lax.ppermute(source, 'layer', [((i + 1) % layers, i) for i in range(layer...]
    psum x1 -> x0, blocking collectives: 17.4 us -> none  [shards(): band_total = lax.psum(jnp.sum(powers, axis=1), 'freq')]
    all_to_all x0 -> x2, starting transfers between devices: none -> 14.9 us  [the longest x1 8.95 us: shards(): lax.all_to_all(chosen(place, source, above), ('block', 'freq'), 0, 0)]
    pallas_call x0 -> x4, Pallas kernels: none -> 13 us  [the longest x1 8.57 us: correlations_of(): pl.pallas_call(correlate, out_shape=jax.ShapeDtypeStruct((stations, SHIFT...]
    unnamed x8, local copies, waits for them, and re-layouts: 0.96 us -> 4.13 us
  transfers between devices with their start and end apart: 5 -> 3, of which waited for: 1 -> 2; matrix products, arithmetic and copies ran while one was open for 29% -> 2% of each run, Pallas kernels for 0% -> 4%
where the time goes in v1:
time: 48.9 us; the launch traced here: 48.4 us
  starting transfers between devices  26 us (53%)
  Pallas kernels  13 us (27%)
  waiting for transfers between devices  4.37 us (9%)
  local copies, waits for them, and re-layouts  4.21 us (9%)
  other arithmetic  0.71 us (1%)
    ppermute x1, starting transfers between devices, shards(): lax.ppermute(source, 'layer', [((i + 1) % layers, i) for i in range(layer...  11.1 us
    all_to_all x1, starting transfers between devices, shards(): lax.all_to_all(chosen(place, source, above), ('block', 'freq'), 0, 0)  8.95 us
    pallas_call x1, Pallas kernels, correlations_of(): pl.pallas_call(correlate, out_shape=jax.ShapeDtypeStruct((stations, SHIFT...  8.57 us
    all_to_all x1, starting transfers between devices, shards(): own = lax.all_to_all(repeated, 'freq', 0, 0)  5.96 us
    unnamed x8, local copies, waits for them, and re-layouts  4.13 us
    all_to_all x1, waiting for transfers between devices, shards(): lax.all_to_all(chosen(place, source, above), ('block', 'freq'), 0, 0)  2.74 us
    pallas_call x1, Pallas kernels, whitened_block(): pl.pallas_call(whiten, out_shape=[jax.ShapeDtypeStruct((stations, F), jnp...  1.91 us
    pallas_call x1, Pallas kernels, prepared(): pl.pallas_call(prepare, out_shape=[jax.ShapeDtypeStruct((bands,) + spectr...  1.82 us
  transfers between devices with their start and end apart: 3, of which 2 were waited for; matrix products, arithmetic and copies ran while one was open for 2% of the time, Pallas kernels for 4%

profile of v1, /device:TPU:1, one launch (start us, length us, event | category | flops | bytes accessed | tf_op | source)
XLA Modules:
  0.0 48.4 jit_solution(5870941479169510884)
XLA Ops:
  0.0 1.8 %shard_map.64 = (bf16[8,2,64,256]{3,2,1,0:T(8,128)(2,1)}, bf16[8,16,256]{2,1,0:T(8,128)(2,1)}) custom-call(bf16[2,64,256]{2,1,0:T(8,128)(2,1)} %spectra_hbm.1, s32[1,64]{1,0:T(1,128)} %bitcast.4), custom_call_target="tpu_custom_call" | custom-call | flops 32768 | bytes 655360 | tf_op jit(solution)/shard_map/pallas_call | solution.py:80
  1.8 6.0 %all-to-all-start = ((bf16[8,2,64,256]{3,2,1,0:T(8,128)(2,1)}), bf16[8,2,64,256]{3,2,1,0:T(8,128)(2,1)S(1)}, u32[]{:S(2)}, u32[]{:S(2)}) async-start(bf16[8,2,64,256]{3,2,1,0:T(8,128)(2,1)} %get-tuple-element.15), calls=%async_computation | async-start | bytes 1048576 | tf_op jit(solution)/shard_map/all_to_all | solution.py:263
  7.8 11.1 %collective-permute-start = (bf16[8,16,256]{2,1,0:T(8,128)(2,1)}, bf16[8,16,256]{2,1,0:T(8,128)(2,1)S(1)}, u32[]{:S(2)}, u32[]{:S(2)}) collective-permute-start(bf16[8,16,256]{2,1,0:T(8,128)(2,1)} %get-tuple-element.14.source_ref), channel_id=1, source_target_pairs={{32,0},{64,32},{96,64},{128,96},{160,128},{192,160},{224,192},{256... | collective-permute-start | bytes 196616 | tf_op jit(solution)/shard_map/ppermute | solution.py:264
  18.9 1.6 %collective-permute-done.above_ref = bf16[8,16,256]{2,1,0:T(8,128)(2,1)S(1)} collective-permute-done((bf16[8,16,256]{2,1,0:T(8,128)(2,1)}, bf16[8,16,256]{2,1,0:T(8,128)(2,1)S(1)}, u32[]{:S(2)}, u32[]{:S(2)}) %collective-permute-start) | collective-permute-done | bytes 65568 | tf_op jit(solution)/shard_map/ppermute | solution.py:264
  20.5 0.0 all-to-all-done.own_ref
  20.5 0.0 copy-start.2
  20.5 0.8 %copy-done.2 = bf16[8,16,256]{2,1,0:T(8,128)(2,1)S(1)} copy-done((bf16[8,16,256]{2,1,0:T(8,128)(2,1)S(1)}, bf16[8,16,256]{2,1,0:T(8,128)(2,1)}, u32[]{:S(2)}) %copy-start.2) | copy-done | bytes 65560
  21.4 0.7 %shard_map.66 = bf16[32,16,256]{2,1,0:T(8,128)(2,1)} custom-call(s32[1]{0:T(128)} %bitcast.place_ref, bf16[8,16,256]{2,1,0:T(8,128)(2,1)S(1)} %copy-done.2, bf16[8,16,256]{2,1,0:T(8,128)(2,1)S(1)} %collective-permute-done.above_ref), custom_call_target="tpu_custom_call" | custom-call | bytes 393216 | tf_op jit(solution)/shard_map/pallas_call | solution.py:114
  22.1 8.9 %all-to-all-start.1 = ((bf16[32,16,256]{2,1,0:T(8,128)(2,1)}), bf16[32,16,256]{2,1,0:T(8,128)(2,1)S(1)}, u32[]{:S(2)}, u32[]{:S(2)}) async-start(bf16[32,16,256]{2,1,0:T(8,128)(2,1)} %shard_map.66), calls=%async_computation.1 | async-start | bytes 524288 | tf_op jit(solution)/shard_map/all_to_all | solution.py:267
  31.1 0.7 %multiply_bitcast_fusion = f32[64,24]{0,1:T(8,128)S(1)} fusion(s32[64,3,8]{0,2,1:T(8,128)} %param.8), kind=kLoop, calls=%fused_computation | loop fusion | flops 3072 | bytes 12288 | tf_op jit(solution)/shard_map/mul | solution.py:268
  31.8 0.1 copy.8.mask_ref
  31.9 0.0 copy-start
  31.9 1.2 %copy-done = bf16[2048,256]{1,0:T(8,128)(2,1)S(1)} copy-done((bf16[2048,256]{1,0:T(8,128)(2,1)S(1)}, bf16[2048,256]{1,0:T(8,128)(2,1)}, u32[]{:S(2)}) %copy-start) | copy-done | bytes 1048600
  33.1 0.0 copy-start.1
  33.1 1.2 %copy-done.1 = bf16[2048,256]{1,0:T(8,128)(2,1)S(1)} copy-done((bf16[2048,256]{1,0:T(8,128)(2,1)S(1)}, bf16[2048,256]{1,0:T(8,128)(2,1)}, u32[]{:S(2)}) %copy-start.1) | copy-done | bytes 1048600
  34.3 0.0 copy-start.3
  34.3 0.8 %copy-done.3 = f32[8,2048]{1,0:T(8,128)S(1)} copy-done((f32[8,2048]{1,0:T(8,128)S(1)}, f32[8,2048]{1,0:T(8,128)}, u32[]{:S(2)}) %copy-start.3) | copy-done | bytes 65560
  35.2 1.9 %shard_map.65 = (bf16[64,2048]{1,0:T(8,128)(2,1)S(1)}, bf16[64,2048]{1,0:T(8,128)(2,1)S(1)}, bf16[2048,256]{1,0:T(8,128)(2,1)S(1)}, bf16[2048,256]{1,0:T(8,128)(2,1)S(1)}, f32[8,2048]{1,0:T(8,128)S(1)}) custom-call(bf16[8,2,64,256]{3,2,1,0:T(8,128)(2,1)S(1)} %all-to-all-done.own_ref, bf16[2048,256]{1,0:T(8,128)(2,1)S(1)} %copy-done.1, ...), custom_call_target="tpu_custom_call" | custom-call | flops 3932160 | bytes 1048576 | tf_op jit(solution)/shard_map/pallas_call | solution.py:149
  37.1 2.7 %all-to-all-done.1.part_ref = bf16[32,16,256]{2,1,0:T(8,128)(2,1)S(1)} async-done(((bf16[32,16,256]{2,1,0:T(8,128)(2,1)}), bf16[32,16,256]{2,1,0:T(8,128)(2,1)S(1)}, u32[]{:S(2)}, u32[]{:S(2)}) %all-to-all-start.1) | async-done | bytes 262176 | tf_op jit(solution)/shard_map/all_to_all | solution.py:267
  39.8 8.6 %shard_map.67 = f32[64,3,8,512]{3,2,1,0:T(8,128)} custom-call(s32[1]{0:T(128)} %bitcast.place_ref, bf16[64,2048]{1,0:T(8,128)(2,1)S(1)} %get-tuple-element.17.own_real, bf16[64,2048]{1,0:T(8,128)(2,1)S(1)} %get-tuple-element.18.own_imag, bf16[2048,256]{1,0:T(8,128)(2,1)S(1)} %get-tuple-element.19.cos_ref, bf16[2048,256]{1,0:T(8,128)(2,1)S(1)} %get-tuple-element.20.sin_ref, ...), custom_call_target="tpu_custom_call" | custom-call | flops 3221225472 | bytes 3145728 | tf_op jit(solution)/shard_map/pallas_call | solution.py:236
Async XLA Ops:
  1.8 18.7 %all-to-all-start = ((bf16[8,2,64,256]{3,2,1,0:T(8,128)(2,1)}), bf16[8,2,64,256]{3,2,1,0:T(8,128)(2,1)S(1)}, u32[]{:S(2)}, u32[]{:S(2)}) async-start(bf16[8,2,64,256]{3,2,1,0:T(8,128)(2,1)} %get-tuple-element.15), calls=%async_computation | async-start | bytes 1048576 | tf_op jit(solution)/shard_map/all_to_all | solution.py:263
  7.8 12.7 %collective-permute-start = (bf16[8,16,256]{2,1,0:T(8,128)(2,1)}, bf16[8,16,256]{2,1,0:T(8,128)(2,1)S(1)}, u32[]{:S(2)}, u32[]{:S(2)}) collective-permute-start(bf16[8,16,256]{2,1,0:T(8,128)(2,1)} %get-tuple-element.14.source_ref), channel_id=1, source_target_pairs={{32,0},{64,32},{96,64},{128,96},{160,128},{192,160},{224,192},{256... | collective-permute-start | bytes 196616 | tf_op jit(solution)/shard_map/ppermute | solution.py:264
  20.5 0.8 %copy-start.2 = (bf16[8,16,256]{2,1,0:T(8,128)(2,1)S(1)}, bf16[8,16,256]{2,1,0:T(8,128)(2,1)}, u32[]{:S(2)}) copy-start(bf16[8,16,256]{2,1,0:T(8,128)(2,1)} %get-tuple-element.14.source_ref) | copy-start | bytes 196612
  22.1 17.7 %all-to-all-start.1 = ((bf16[32,16,256]{2,1,0:T(8,128)(2,1)}), bf16[32,16,256]{2,1,0:T(8,128)(2,1)S(1)}, u32[]{:S(2)}, u32[]{:S(2)}) async-start(bf16[32,16,256]{2,1,0:T(8,128)(2,1)} %shard_map.66), calls=%async_computation.1 | async-start | bytes 524288 | tf_op jit(solution)/shard_map/all_to_all | solution.py:267
  31.9 1.2 %copy-start = (bf16[2048,256]{1,0:T(8,128)(2,1)S(1)}, bf16[2048,256]{1,0:T(8,128)(2,1)}, u32[]{:S(2)}) copy-start(bf16[2048,256]{1,0:T(8,128)(2,1)} %constant.14.clone.sin_from) | copy-start | bytes 3145732
  33.1 1.2 %copy-start.1 = (bf16[2048,256]{1,0:T(8,128)(2,1)S(1)}, bf16[2048,256]{1,0:T(8,128)(2,1)}, u32[]{:S(2)}) copy-start(bf16[2048,256]{1,0:T(8,128)(2,1)} %constant.13.clone.cos_from) | copy-start | bytes 3145732
  34.3 0.8 %copy-start.3 = (f32[8,2048]{1,0:T(8,128)S(1)}, f32[8,2048]{1,0:T(8,128)}, u32[]{:S(2)}) copy-start(f32[8,2048]{1,0:T(8,128)} %constant.15.clone.last_from) | copy-start | bytes 196612

commit v2 on v1

--- a/solution.py
+++ b/solution.py
@@ -17,16 +17,26 @@
 LAYER = 4
 epsilon = 1e-06
 MIB = 1024 * 1024
+GROUP = 4
 
 
 def tables():
     bins = np.arange(F, dtype=np.int64)
     taus = np.arange(HALF, dtype=np.int64)
     angles = (bins[:, None] * taus[None, :] % (2 * F)).astype(np.float64) * (math.pi / F)
-    edge = (bins * HALF % (2 * F)).astype(np.float64) * (math.pi / F)
-    bf16 = ml_dtypes.bfloat16
-    last = np.stack([np.cos(edge), np.sin(edge)] * 4).astype(bf16).astype(np.float32)
-    return np.cos(angles).astype(bf16), (-np.sin(angles)).astype(bf16), last
+    return [half.astype(ml_dtypes.bfloat16) for half in (np.cos(angles), -np.sin(angles))]
+
+
+def edge_rows():
+    turn = 2 * F // HALF
+    lane = lax.broadcasted_iota(jnp.int32, (8, 128), 1) % turn
+    cos = sin = jnp.zeros((8, 128), jnp.float32)
+    for r in range(turn):
+        angle = 2 * math.pi * r / turn
+        values = np.array([math.cos(angle), math.sin(angle)]).astype(ml_dtypes.bfloat16)
+        cos = jnp.where(lane == r, float(values[0]), cos)
+        sin = jnp.where(lane == r, float(values[1]), sin)
+    return jnp.concatenate([cos] * (F // 128), axis=1), jnp.concatenate([sin] * (F // 128), axis=1)
 
 
 def whitened(real, imag):
@@ -46,8 +56,7 @@
 
 def prepare(spectra_hbm, ok_hbm, repeated_ref, source_ref, spectra_ref, ok_ref, valid_ref, turned_ref, sems):
     stations = spectra_ref.shape[1]
-    bands, both_rows, _ = source_ref.shape
-    partners = both_rows // 2
+    bands = source_ref.shape[0]
     loads = [pltpu.make_async_copy(spectra_hbm, spectra_ref, sems.at[0]), pltpu.make_async_copy(ok_hbm, ok_ref, sems.at[1])]
     for load in loads:
         load.start()
@@ -64,9 +73,7 @@
     stores = [pltpu.make_async_copy(valid_ref, repeated_ref.at[q], sems.at[2 + q]) for q in range(bands)]
     for store in stores:
         store.start()
-    for q in range(bands):
-        rows = slice(q * partners, (q + 1) * partners)
-        turned_ref[q] = jnp.concatenate([real[rows], imag[rows]], axis=0).astype(jnp.bfloat16)
+    turn(real, imag, turned_ref)
     stores.append(pltpu.make_async_copy(turned_ref, source_ref, sems.at[2 + bands]))
     stores[-1].start()
     for store in stores:
@@ -95,6 +102,14 @@
     )(spectra, station_ok.reshape(1, stations))
 
 
+def turn(real, imag, turned_ref):
+    bands, both_rows, _ = turned_ref.shape
+    partners = both_rows // 2
+    for q in range(bands):
+        rows = slice(q * partners, (q + 1) * partners)
+        turned_ref[q] = jnp.concatenate([real[rows], imag[rows]], axis=0).astype(jnp.bfloat16)
+
+
 def choose(place_ref, source_ref, above_ref, sent_ref):
     bands = source_ref.shape[0]
     for other in range(LAYER):
@@ -121,9 +136,9 @@
     )(place, source, above)
 
 
-def whiten(own_ref, cos_from, sin_from, last_from, real_ref, imag_ref, cos_ref, sin_ref, last_ref, sems):
+def whiten(own_ref, cos_from, sin_from, real_ref, imag_ref, cos_ref, sin_ref, sems):
     bands = own_ref.shape[0]
-    pairs = ((cos_from, cos_ref), (sin_from, sin_ref), (last_from, last_ref))
+    pairs = ((cos_from, cos_ref), (sin_from, sin_ref))
     loads = [pltpu.make_async_copy(table, to, sems.at[i]) for i, (table, to) in enumerate(pairs)]
     for load in loads:
         load.start()
@@ -150,80 +165,101 @@
         whiten,
         out_shape=[jax.ShapeDtypeStruct((stations, F), jnp.bfloat16)] * 2
         + [jax.ShapeDtypeStruct(table.shape, table.dtype) for table in given],
-        in_specs=[vmem] + [pl.BlockSpec(memory_space=pl.ANY)] * 3,
-        out_specs=[vmem] * 5,
-        scratch_shapes=[pltpu.SemaphoreType.DMA((3,))],
+        in_specs=[vmem] + [pl.BlockSpec(memory_space=pl.ANY)] * 2,
+        out_specs=[vmem] * 4,
+        scratch_shapes=[pltpu.SemaphoreType.DMA((2,))],
         compiler_params=pltpu.CompilerParams(vmem_limit_bytes=8 * MIB),
         cost_estimate=pl.CostEstimate(flops=30 * stations * F, bytes_accessed=8 * stations * F, transcendentals=stations * F),
     )(own, *given)
 
 
-def correlate(place_ref, own_real, own_imag, cos_ref, sin_ref, last_ref, part_ref, mask_ref, out_ref,
-              part_real, part_imag, turned, cross_real, cross_imag, lags, sems):
+def correlate(place_ref, own_real, own_imag, cos_ref, sin_ref, part_ref, mask_ref, out_ref,
+              others, cross, lags, sems):
     stations = own_real.shape[0]
     bands = part_ref.shape[0] // LAYER
     partners = part_ref.shape[1] // 2
-    last_cos = last_ref[0:1, :]
-    last_sin = last_ref[1:2, :]
-    for k in range(SHIFTS):
+    last_cos, last_sin = edge_rows()
+    lane = lax.broadcasted_iota(jnp.int32, (stations, 128), 1)
+    mirror = lax.rem(128 - lane, 128)
+    parts_per_shift = partners // GROUP
+    steps = [(k, g) for k in range(SHIFTS) for g in range(parts_per_shift)]
+
+    def whiten_part(k):
         first = lax.rem(place_ref[0] + (k + 1), LAYER) * bands
         both = jnp.concatenate([part_ref[first + q] for q in range(bands)], axis=1).astype(jnp.float32)
         real, imag = whitened(both[:partners], both[partners:])
         real = real.astype(jnp.bfloat16).astype(jnp.float32)
         imag = imag.astype(jnp.bfloat16).astype(jnp.float32)
-        part_real[k * partners:(k + 1) * partners, :] = real
-        part_imag[k * partners:(k + 1) * partners, :] = imag
-        turned[0, k * partners:(k + 1) * partners, :] = real * last_cos - imag * last_sin
-        turned[1, k * partners:(k + 1) * partners, :] = imag * last_cos + real * last_sin
-
-    edge = jnp.zeros((stations, SHIFTS * partners), jnp.float32)
-    for c, own in ((0, own_real), (1, own_imag)):
-        high = turned[c].astype(jnp.bfloat16)
-        low = (turned[c] - high.astype(jnp.float32)).astype(jnp.bfloat16)
-        for part in (high, low):
-            edge = edge + lax.dot_general(own[...], part, (((1,), (1,)), ((), ())),
+        others[k, 0] = real
+        others[k, 1] = imag
+        edge = jnp.zeros((stations, partners), jnp.float32)
+        for own, turned in ((own_real, real * last_cos - imag * last_sin), (own_imag, imag * last_cos + real * last_sin)):
+            edge = edge + lax.dot_general(own[...], turned.astype(jnp.bfloat16), (((1,), (1,)), ((), ())),
                                           preferred_element_type=jnp.float32)
-    edge = edge * mask_ref[...]
+        return edge * mask_ref[:, k * partners:(k + 1) * partners]
+
+    def form(n):
+        k, g = steps[n]
+        for p in range(GROUP):
+            j = g * GROUP + p
+            other_real = jnp.broadcast_to(others[k, 0, j:j + 1, :], (16, F)).astype(jnp.bfloat16)
+            other_imag = jnp.broadcast_to(others[k, 1, j:j + 1, :], (16, F)).astype(jnp.bfloat16)
+            for i in range(stations // 16):
+                real = own_real[i * 16:(i + 1) * 16, :]
+                imag = own_imag[i * 16:(i + 1) * 16, :]
+                at = slice(p * stations + i * 16, p * stations + (i + 1) * 16)
+                cross[n % 2, 0, at, :] = real * other_real + imag * other_imag
+                cross[n % 2, 1, at, :] = imag * other_real - real * other_imag
+
+    def product(n):
+        return (jnp.dot(cross[n % 2, 0], cos_ref[...], preferred_element_type=jnp.float32),
+                jnp.dot(cross[n % 2, 1], sin_ref[...], preferred_element_type=jnp.float32))
 
     def finished(k, q):
         rows = lags.at[k, q].reshape(stations, partners, 128)
         return pltpu.make_async_copy(rows, out_ref.at[:, k, :, pl.ds(q * 128, 128)], sems.at[k, q])
 
-    lane = lax.broadcasted_iota(jnp.int32, (stations, 128), 1)
-    mirror = lax.rem(128 - lane, 128)
-    for k in range(SHIFTS):
-        def cross(j, carry):
-            row = k * partners + j
-            at = pl.ds(pl.multiple_of(j * stations, 16), stations)
-            other_real = jnp.broadcast_to(part_real[pl.ds(row, 1), :], (16, F)).astype(jnp.bfloat16)
-            other_imag = jnp.broadcast_to(part_imag[pl.ds(row, 1), :], (16, F)).astype(jnp.bfloat16)
-            for g in range(stations // 16):
-                real = own_real[g * 16:(g + 1) * 16, :]
-                imag = own_imag[g * 16:(g + 1) * 16, :]
-                at = pl.ds(pl.multiple_of(j * stations + g * 16, 16), 16)
-                cross_real[at, :] = real * other_real + imag * other_imag
-                cross_imag[at, :] = imag * other_real - real * other_imag
-            return carry
-
-        lax.fori_loop(0, partners, cross, 0)
-        even = jnp.dot(cross_real[...], cos_ref[...], preferred_element_type=jnp.float32)
-        odd = jnp.dot(cross_imag[...], sin_ref[...], preferred_element_type=jnp.float32)
-        for j in range(partners):
-            column = k * partners + j
-            weight = mask_ref[:, column:column + 1]
-            c = even[j * stations:(j + 1) * stations, :] * weight
-            s = odd[j * stations:(j + 1) * stations, :] * weight
-            up = c + s
-            down = c - s
-            near, far = down[:, :128], down[:, 128:]
-            ends = jnp.broadcast_to(edge[:, column:column + 1], (stations, 128))
-            first = jnp.take_along_axis(jnp.where(lane == 0, ends, far), mirror, axis=1)
-            second = jnp.take_along_axis(jnp.where(lane == 0, far, near), mirror, axis=1)
-            at = pl.ds(j, stations, stride=partners)
-            for q, piece in enumerate((first, second, up[:, :128], up[:, 128:])):
-                lags[k, q, at, :] = piece
-        for q in range(4):
-            finished(k, q).start()
+    def finish(n, pair, edge):
+        k, g = steps[n]
+        even, odd = pair
+        down = []
+        for half in (0, 1):
+            for p in range(GROUP):
+                j = g * GROUP + p
+                weight = mask_ref[:, k * partners + j:k * partners + j + 1]
+                rows = slice(p * stations, (p + 1) * stations)
+                c = even[rows, half * 128:(half + 1) * 128] * weight
+                s = odd[rows, half * 128:(half + 1) * 128] * weight
+                lags[k, 2 + half, pl.ds(j, stations, stride=partners), :] = c + s
+                down.append(c - s)
+            if g == parts_per_shift - 1:
+                finished(k, 2 + half).start()
+        for half in (0, 1):
+            for p in range(GROUP):
+                j = g * GROUP + p
+                near, far = down[p], down[GROUP + p]
+                if half == 0:
+                    ends = jnp.broadcast_to(edge[:, j:j + 1], (stations, 128))
+                    piece = jnp.where(lane == 0, ends, far)
+                else:
+                    piece = jnp.where(lane == 0, far, near)
+                lags[k, half, pl.ds(j, stations, stride=partners), :] = jnp.take_along_axis(piece, mirror, axis=1)
+            if g == parts_per_shift - 1:
+                finished(k, half).start()
+
+    edges = [whiten_part(0)]
+    form(0)
+    before = None
+    for n in range(len(steps)):
+        pair = product(n)
+        if n + 1 < len(steps):
+            if steps[n + 1][1] == 0:
+                edges.append(whiten_part(steps[n + 1][0]))
+            form(n + 1)
+        if before is not None:
+            finish(n - 1, before, edges[steps[n - 1][0]])
+        before = pair
+    finish(len(steps) - 1, before, edges[-1])
     for k in range(SHIFTS):
         for q in range(4):
             finished(k, q).wait()
@@ -236,14 +272,11 @@
     return pl.pallas_call(
         correlate,
         out_shape=jax.ShapeDtypeStruct((stations, SHIFTS, partners, L), jnp.float32),
-        in_specs=[pl.BlockSpec(memory_space=pltpu.SMEM)] + [vmem] * 7,
+        in_specs=[pl.BlockSpec(memory_space=pltpu.SMEM)] + [vmem] * 6,
         out_specs=pl.BlockSpec(memory_space=pl.ANY),
         scratch_shapes=[
-            pltpu.VMEM((SHIFTS * partners, F), jnp.float32),
-            pltpu.VMEM((SHIFTS * partners, F), jnp.float32),
-            pltpu.VMEM((2, SHIFTS * partners, F), jnp.float32),
-            pltpu.VMEM((stations * partners, F), jnp.bfloat16),
-            pltpu.VMEM((stations * partners, F), jnp.bfloat16),
+            pltpu.VMEM((SHIFTS, 2, partners, F), jnp.float32),
+            pltpu.VMEM((2, 2, GROUP * stations, F), jnp.bfloat16),
             pltpu.VMEM((SHIFTS, L // 128, stations * partners, 128), jnp.float32),
             pltpu.SemaphoreType.DMA((SHIFTS, L // 128)),
         ],

time: 48.9 us -> 46 us (0.941)
  Pallas kernels: 13 us -> 10 us
  waiting for transfers between devices: 4.37 us -> 5.3 us
  local copies, waits for them, and re-layouts: 4.21 us -> 3.38 us
    pallas_call x1, Pallas kernels: 8.57 us -> 5.67 us  [correlations_of(): pl.pallas_call(correlate, out_shape=jax.ShapeDtypeStruct((stations, SHIFT...]
    all_to_all x1, waiting for transfers between devices: 2.74 us -> 3.67 us  [shards(): lax.all_to_all(chosen(place, source, above), ('block', 'freq'), 0, 0)]
    unnamed x8 -> x6, local copies, waits for them, and re-layouts: 4.13 us -> 3.29 us
where the time goes in v2:
time: 46 us; the launch traced here: 45.5 us
  starting transfers between devices  26 us (57%)
  Pallas kernels  10 us (22%)
  waiting for transfers between devices  5.3 us (12%)
  local copies, waits for them, and re-layouts  3.38 us (7%)
  other arithmetic  0.71 us (2%)
    ppermute x1, starting transfers between devices, shards(): lax.ppermute(source, 'layer', [((i + 1) % layers, i) for i in range(layer...  11.1 us
    all_to_all x1, starting transfers between devices, shards(): lax.all_to_all(chosen(place, source, above), ('block', 'freq'), 0, 0)  8.95 us
    all_to_all x1, starting transfers between devices, shards(): own = lax.all_to_all(repeated, 'freq', 0, 0)  5.96 us
    pallas_call x1, Pallas kernels, correlations_of(): pl.pallas_call(correlate, out_shape=jax.ShapeDtypeStruct((stations, SHIFT...  5.67 us
    all_to_all x1, waiting for transfers between devices, shards(): lax.all_to_all(chosen(place, source, above), ('block', 'freq'), 0, 0)  3.67 us
    unnamed x6, local copies, waits for them, and re-layouts  3.29 us
    pallas_call x1, Pallas kernels, whitened_block(): pl.pallas_call(whiten, out_shape=[jax.ShapeDtypeStruct((stations, F), jnp...  1.82 us
    pallas_call x1, Pallas kernels, prepared(): pl.pallas_call(prepare, out_shape=[jax.ShapeDtypeStruct((bands,) + spectr...  1.81 us
  transfers between devices with their start and end apart: 3, of which 2 were waited for; matrix products, arithmetic and copies ran while one was open for 2% of the time, Pallas kernels for 4%

profile of v2, /device:TPU:1, one launch (start us, length us, event | category | flops | bytes accessed | tf_op | source)
XLA Modules:
  0.0 45.5 jit_solution(13097681900710039746)
XLA Ops:
  0.0 1.8 %shard_map.55 = (bf16[8,2,64,256]{3,2,1,0:T(8,128)(2,1)}, bf16[8,16,256]{2,1,0:T(8,128)(2,1)}) custom-call(bf16[2,64,256]{2,1,0:T(8,128)(2,1)} %spectra_hbm.1, s32[1,64]{1,0:T(1,128)} %bitcast.4), custom_call_target="tpu_custom_call" | custom-call | flops 32768 | bytes 655360 | tf_op jit(solution)/shard_map/pallas_call | solution.py:87
  1.8 6.0 %all-to-all-start = ((bf16[8,2,64,256]{3,2,1,0:T(8,128)(2,1)}), bf16[8,2,64,256]{3,2,1,0:T(8,128)(2,1)S(1)}, u32[]{:S(2)}, u32[]{:S(2)}) async-start(bf16[8,2,64,256]{3,2,1,0:T(8,128)(2,1)} %get-tuple-element.14), calls=%async_computation | async-start | bytes 1048576 | tf_op jit(solution)/shard_map/all_to_all | solution.py:296
  7.8 11.1 %collective-permute-start = (bf16[8,16,256]{2,1,0:T(8,128)(2,1)}, bf16[8,16,256]{2,1,0:T(8,128)(2,1)S(1)}, u32[]{:S(2)}, u32[]{:S(2)}) collective-permute-start(bf16[8,16,256]{2,1,0:T(8,128)(2,1)} %get-tuple-element.13.source_ref), channel_id=1, source_target_pairs={{32,0},{64,32},{96,64},{128,96},{160,128},{192,160},{224,192},{256... | collective-permute-start | bytes 196616 | tf_op jit(solution)/shard_map/ppermute | solution.py:297
  18.9 1.6 %collective-permute-done.above_ref = bf16[8,16,256]{2,1,0:T(8,128)(2,1)S(1)} collective-permute-done((bf16[8,16,256]{2,1,0:T(8,128)(2,1)}, bf16[8,16,256]{2,1,0:T(8,128)(2,1)S(1)}, u32[]{:S(2)}, u32[]{:S(2)}) %collective-permute-start) | collective-permute-done | bytes 65568 | tf_op jit(solution)/shard_map/ppermute | solution.py:297
  20.5 0.0 all-to-all-done.own_ref
  20.5 0.0 copy-start.2
  20.5 0.8 %copy-done.2 = bf16[8,16,256]{2,1,0:T(8,128)(2,1)S(1)} copy-done((bf16[8,16,256]{2,1,0:T(8,128)(2,1)S(1)}, bf16[8,16,256]{2,1,0:T(8,128)(2,1)}, u32[]{:S(2)}) %copy-start.2) | copy-done | bytes 65560
  21.4 0.7 %shard_map.57 = bf16[32,16,256]{2,1,0:T(8,128)(2,1)} custom-call(s32[1]{0:T(128)} %bitcast.place_ref, bf16[8,16,256]{2,1,0:T(8,128)(2,1)S(1)} %copy-done.2, bf16[8,16,256]{2,1,0:T(8,128)(2,1)S(1)} %collective-permute-done.above_ref), custom_call_target="tpu_custom_call" | custom-call | bytes 393216 | tf_op jit(solution)/shard_map/pallas_call | solution.py:129
  22.1 8.9 %all-to-all-start.1 = ((bf16[32,16,256]{2,1,0:T(8,128)(2,1)}), bf16[32,16,256]{2,1,0:T(8,128)(2,1)S(1)}, u32[]{:S(2)}, u32[]{:S(2)}) async-start(bf16[32,16,256]{2,1,0:T(8,128)(2,1)} %shard_map.57), calls=%async_computation.1 | async-start | bytes 524288 | tf_op jit(solution)/shard_map/all_to_all | solution.py:300
  31.1 0.7 %multiply_bitcast_fusion = f32[64,24]{0,1:T(8,128)S(1)} fusion(s32[64,3,8]{0,2,1:T(8,128)} %param.7), kind=kLoop, calls=%fused_computation | loop fusion | flops 3072 | bytes 12288 | tf_op jit(solution)/shard_map/mul | solution.py:301
  31.8 0.1 copy.7.mask_ref
  31.9 0.0 copy-start
  31.9 1.2 %copy-done = bf16[2048,256]{1,0:T(8,128)(2,1)S(1)} copy-done((bf16[2048,256]{1,0:T(8,128)(2,1)S(1)}, bf16[2048,256]{1,0:T(8,128)(2,1)}, u32[]{:S(2)}) %copy-start) | copy-done | bytes 1048600
  33.1 0.0 copy-start.1
  33.1 1.2 %copy-done.1 = bf16[2048,256]{1,0:T(8,128)(2,1)S(1)} copy-done((bf16[2048,256]{1,0:T(8,128)(2,1)S(1)}, bf16[2048,256]{1,0:T(8,128)(2,1)}, u32[]{:S(2)}) %copy-start.1) | copy-done | bytes 1048600
  34.3 1.8 %shard_map.56 = (bf16[64,2048]{1,0:T(8,128)(2,1)S(1)}, bf16[64,2048]{1,0:T(8,128)(2,1)S(1)}, bf16[2048,256]{1,0:T(8,128)(2,1)S(1)}, bf16[2048,256]{1,0:T(8,128)(2,1)S(1)}) custom-call(bf16[8,2,64,256]{3,2,1,0:T(8,128)(2,1)S(1)} %all-to-all-done.own_ref, bf16[2048,256]{1,0:T(8,128)(2,1)S(1)} %copy-done.1, bf16[2048,256]{1,0:T(8,128)(2,1)S(1)} %copy-done), custom_call_target="tpu_custom_call" | custom-call | flops 3932160 | bytes 1048576 | tf_op jit(solution)/shard_map/pallas_call | solution.py:164
  36.1 3.7 %all-to-all-done.1.part_ref = bf16[32,16,256]{2,1,0:T(8,128)(2,1)S(1)} async-done(((bf16[32,16,256]{2,1,0:T(8,128)(2,1)}), bf16[32,16,256]{2,1,0:T(8,128)(2,1)S(1)}, u32[]{:S(2)}, u32[]{:S(2)}) %all-to-all-start.1) | async-done | bytes 262176 | tf_op jit(solution)/shard_map/all_to_all | solution.py:300
  39.8 5.7 %shard_map.58 = f32[64,3,8,512]{3,2,1,0:T(8,128)} custom-call(s32[1]{0:T(128)} %bitcast.place_ref, bf16[64,2048]{1,0:T(8,128)(2,1)S(1)} %get-tuple-element.16.own_real, bf16[64,2048]{1,0:T(8,128)(2,1)S(1)} %get-tuple-element.17.own_imag, bf16[2048,256]{1,0:T(8,128)(2,1)S(1)} %get-tuple-element.18.cos_ref, bf16[2048,256]{1,0:T(8,128)(2,1)S(1)} %get-tuple-element.19.sin_ref, ...), custom_call_target="tpu_custom_call" | custom-call | flops 3221225472 | bytes 3145728 | tf_op jit(solution)/shard_map/pallas_call | solution.py:272
Async XLA Ops:
  1.8 18.7 %all-to-all-start = ((bf16[8,2,64,256]{3,2,1,0:T(8,128)(2,1)}), bf16[8,2,64,256]{3,2,1,0:T(8,128)(2,1)S(1)}, u32[]{:S(2)}, u32[]{:S(2)}) async-start(bf16[8,2,64,256]{3,2,1,0:T(8,128)(2,1)} %get-tuple-element.14), calls=%async_computation | async-start | bytes 1048576 | tf_op jit(solution)/shard_map/all_to_all | solution.py:296
  7.8 12.7 %collective-permute-start = (bf16[8,16,256]{2,1,0:T(8,128)(2,1)}, bf16[8,16,256]{2,1,0:T(8,128)(2,1)S(1)}, u32[]{:S(2)}, u32[]{:S(2)}) collective-permute-start(bf16[8,16,256]{2,1,0:T(8,128)(2,1)} %get-tuple-element.13.source_ref), channel_id=1, source_target_pairs={{32,0},{64,32},{96,64},{128,96},{160,128},{192,160},{224,192},{256... | collective-permute-start | bytes 196616 | tf_op jit(solution)/shard_map/ppermute | solution.py:297
  20.5 0.8 %copy-start.2 = (bf16[8,16,256]{2,1,0:T(8,128)(2,1)S(1)}, bf16[8,16,256]{2,1,0:T(8,128)(2,1)}, u32[]{:S(2)}) copy-start(bf16[8,16,256]{2,1,0:T(8,128)(2,1)} %get-tuple-element.13.source_ref) | copy-start | bytes 196612
  22.1 17.7 %all-to-all-start.1 = ((bf16[32,16,256]{2,1,0:T(8,128)(2,1)}), bf16[32,16,256]{2,1,0:T(8,128)(2,1)S(1)}, u32[]{:S(2)}, u32[]{:S(2)}) async-start(bf16[32,16,256]{2,1,0:T(8,128)(2,1)} %shard_map.57), calls=%async_computation.1 | async-start | bytes 524288 | tf_op jit(solution)/shard_map/all_to_all | solution.py:300
  31.9 1.2 %copy-start = (bf16[2048,256]{1,0:T(8,128)(2,1)S(1)}, bf16[2048,256]{1,0:T(8,128)(2,1)}, u32[]{:S(2)}) copy-start(bf16[2048,256]{1,0:T(8,128)(2,1)} %constant.12.clone.sin_from) | copy-start | bytes 3145732
  33.1 1.2 %copy-start.1 = (bf16[2048,256]{1,0:T(8,128)(2,1)S(1)}, bf16[2048,256]{1,0:T(8,128)(2,1)}, u32[]{:S(2)}) copy-start(bf16[2048,256]{1,0:T(8,128)(2,1)} %constant.11.clone.cos_from) | copy-start | bytes 3145732

commit v3 on v2

--- a/solution.py
+++ b/solution.py
@@ -17,7 +17,7 @@
 LAYER = 4
 epsilon = 1e-06
 MIB = 1024 * 1024
-GROUP = 4
+ROWS = 32
 
 
 def tables():
@@ -110,6 +110,22 @@
         turned_ref[q] = jnp.concatenate([real[rows], imag[rows]], axis=0).astype(jnp.bfloat16)
 
 
+def stage(source_ref, staged_ref):
+    staged_ref[...] = source_ref[...]
+
+
+def staged(source):
+    vmem = pl.BlockSpec(memory_space=pltpu.VMEM)
+    return pl.pallas_call(
+        stage,
+        out_shape=jax.ShapeDtypeStruct(source.shape, source.dtype),
+        in_specs=[vmem],
+        out_specs=vmem,
+        compiler_params=pltpu.CompilerParams(vmem_limit_bytes=8 * MIB),
+        cost_estimate=pl.CostEstimate(flops=0, bytes_accessed=4 * source.size, transcendentals=0),
+    )(source)
+
+
 def choose(place_ref, source_ref, above_ref, sent_ref):
     bands = source_ref.shape[0]
     for other in range(LAYER):
@@ -179,10 +195,9 @@
     bands = part_ref.shape[0] // LAYER
     partners = part_ref.shape[1] // 2
     last_cos, last_sin = edge_rows()
-    lane = lax.broadcasted_iota(jnp.int32, (stations, 128), 1)
+    lane = lax.broadcasted_iota(jnp.int32, (ROWS, 128), 1)
     mirror = lax.rem(128 - lane, 128)
-    parts_per_shift = partners // GROUP
-    steps = [(k, g) for k in range(SHIFTS) for g in range(parts_per_shift)]
+    steps = [(k, slice(i, i + ROWS)) for k in range(SHIFTS) for i in range(0, stations, ROWS)]
 
     def whiten_part(k):
         first = lax.rem(place_ref[0] + (k + 1), LAYER) * bands
@@ -190,8 +205,9 @@
         real, imag = whitened(both[:partners], both[partners:])
         real = real.astype(jnp.bfloat16).astype(jnp.float32)
         imag = imag.astype(jnp.bfloat16).astype(jnp.float32)
-        others[k, 0] = real
-        others[k, 1] = imag
+        for j in range(partners):
+            others[k % 2, 0, j] = jnp.broadcast_to(real[j:j + 1], (16, F)).astype(jnp.bfloat16)
+            others[k % 2, 1, j] = jnp.broadcast_to(imag[j:j + 1], (16, F)).astype(jnp.bfloat16)
         edge = jnp.zeros((stations, partners), jnp.float32)
         for own, turned in ((own_real, real * last_cos - imag * last_sin), (own_imag, imag * last_cos + real * last_sin)):
             edge = edge + lax.dot_general(own[...], turned.astype(jnp.bfloat16), (((1,), (1,)), ((), ())),
@@ -199,15 +215,13 @@
         return edge * mask_ref[:, k * partners:(k + 1) * partners]
 
     def form(n):
-        k, g = steps[n]
-        for p in range(GROUP):
-            j = g * GROUP + p
-            other_real = jnp.broadcast_to(others[k, 0, j:j + 1, :], (16, F)).astype(jnp.bfloat16)
-            other_imag = jnp.broadcast_to(others[k, 1, j:j + 1, :], (16, F)).astype(jnp.bfloat16)
-            for i in range(stations // 16):
-                real = own_real[i * 16:(i + 1) * 16, :]
-                imag = own_imag[i * 16:(i + 1) * 16, :]
-                at = slice(p * stations + i * 16, p * stations + (i + 1) * 16)
+        k, rows = steps[n]
+        for j in range(partners):
+            for i in range(0, ROWS, 16):
+                real = own_real[rows.start + i:rows.start + i + 16, :]
+                imag = own_imag[rows.start + i:rows.start + i + 16, :]
+                other_real, other_imag = others[k % 2, 0, j], others[k % 2, 1, j]
+                at = slice(j * ROWS + i, j * ROWS + i + 16)
                 cross[n % 2, 0, at, :] = real * other_real + imag * other_imag
                 cross[n % 2, 1, at, :] = imag * other_real - real * other_imag
 
@@ -215,37 +229,36 @@
         return (jnp.dot(cross[n % 2, 0], cos_ref[...], preferred_element_type=jnp.float32),
                 jnp.dot(cross[n % 2, 1], sin_ref[...], preferred_element_type=jnp.float32))
 
-    def finished(k, q):
-        rows = lags.at[k, q].reshape(stations, partners, 128)
-        return pltpu.make_async_copy(rows, out_ref.at[:, k, :, pl.ds(q * 128, 128)], sems.at[k, q])
+    def finished(n, q):
+        k, rows = steps[n]
+        ready = lags.at[n, q].reshape(ROWS, partners, 128)
+        return pltpu.make_async_copy(ready, out_ref.at[pl.ds(rows.start, ROWS), k, :, pl.ds(q * 128, 128)], sems.at[n, q])
 
     def finish(n, pair, edge):
-        k, g = steps[n]
+        k, rows = steps[n]
         even, odd = pair
         down = []
         for half in (0, 1):
-            for p in range(GROUP):
-                j = g * GROUP + p
-                weight = mask_ref[:, k * partners + j:k * partners + j + 1]
-                rows = slice(p * stations, (p + 1) * stations)
-                c = even[rows, half * 128:(half + 1) * 128] * weight
-                s = odd[rows, half * 128:(half + 1) * 128] * weight
-                lags[k, 2 + half, pl.ds(j, stations, stride=partners), :] = c + s
+            for j in range(partners):
+                weight = mask_ref[rows, k * partners + j:k * partners + j + 1]
+                at = slice(j * ROWS, (j + 1) * ROWS)
+                c = even[at, half * 128:(half + 1) * 128] * weight
+                s = odd[at, half * 128:(half + 1) * 128] * weight
+                lags[n, 2 + half, pl.ds(j, ROWS, stride=partners), :] = c + s
                 down.append(c - s)
-            if g == parts_per_shift - 1:
-                finished(k, 2 + half).start()
         for half in (0, 1):
-            for p in range(GROUP):
-                j = g * GROUP + p
-                near, far = down[p], down[GROUP + p]
+            for j in range(partners):
+                near, far = down[j], down[partners + j]
                 if half == 0:
-                    ends = jnp.broadcast_to(edge[:, j:j + 1], (stations, 128))
+                    ends = jnp.broadcast_to(edge[rows, j:j + 1], (ROWS, 128))
                     piece = jnp.where(lane == 0, ends, far)
                 else:
                     piece = jnp.where(lane == 0, far, near)
-                lags[k, half, pl.ds(j, stations, stride=partners), :] = jnp.take_along_axis(piece, mirror, axis=1)
-            if g == parts_per_shift - 1:
-                finished(k, half).start()
+                lags[n, half, pl.ds(j, ROWS, stride=partners), :] = jnp.take_along_axis(piece, mirror, axis=1)
+
+    def send(n):
+        for q in range(4):
+            finished(n, q).start()
 
     edges = [whiten_part(0)]
     form(0)
@@ -253,16 +266,18 @@
     for n in range(len(steps)):
         pair = product(n)
         if n + 1 < len(steps):
-            if steps[n + 1][1] == 0:
-                edges.append(whiten_part(steps[n + 1][0]))
+            if steps[n + 1][0] == len(edges):
+                edges.append(whiten_part(len(edges)))
             form(n + 1)
         if before is not None:
             finish(n - 1, before, edges[steps[n - 1][0]])
+            send(n - 1)
         before = pair
     finish(len(steps) - 1, before, edges[-1])
-    for k in range(SHIFTS):
+    send(len(steps) - 1)
+    for n in range(len(steps)):
         for q in range(4):
-            finished(k, q).wait()
+            finished(n, q).wait()
 
 
 def correlations_of(place, own, parts, mask):
@@ -275,10 +290,10 @@
         in_specs=[pl.BlockSpec(memory_space=pltpu.SMEM)] + [vmem] * 6,
         out_specs=pl.BlockSpec(memory_space=pl.ANY),
         scratch_shapes=[
-            pltpu.VMEM((SHIFTS, 2, partners, F), jnp.float32),
-            pltpu.VMEM((2, 2, GROUP * stations, F), jnp.bfloat16),
-            pltpu.VMEM((SHIFTS, L // 128, stations * partners, 128), jnp.float32),
-            pltpu.SemaphoreType.DMA((SHIFTS, L // 128)),
+            pltpu.VMEM((2, 2, partners, 16, F), jnp.bfloat16),
+            pltpu.VMEM((2, 2, partners * ROWS, F), jnp.bfloat16),
+            pltpu.VMEM((SHIFTS * stations // ROWS, L // 128, partners * ROWS, 128), jnp.float32),
+            pltpu.SemaphoreType.DMA((SHIFTS * stations // ROWS, L // 128)),
         ],
         compiler_params=pltpu.CompilerParams(vmem_limit_bytes=24 * MIB),
         cost_estimate=pl.CostEstimate(
@@ -297,7 +312,7 @@
     above = lax.ppermute(source, "layer", [((i + 1) % layers, i) for i in range(layers)])
     above, own = lax.optimization_barrier((above, own))
     place = lax.axis_index("block").reshape(1)
-    parts = lax.all_to_all(chosen(place, source, above), ("block", "freq"), 0, 0)
+    parts = lax.all_to_all(chosen(place, staged(source), above), ("block", "freq"), 0, 0)
     mask = pair_mask.reshape(stations, SHIFTS * partners).astype(jnp.float32) * (1.0 / math.sqrt(F))
     return correlations_of(place, whitened_block(own), parts, mask)
 

time: 46 us -> 45 us (0.978)
  waiting for transfers between devices: 5.3 us -> 4.45 us
    ppermute x1, waiting for transfers between devices: 1.62 us -> 0.77 us  [shards(): lax.ppermute(source, 'layer', [((i + 1) % layers, i) for i in range(layer...]
where the time goes in v3:
time: 45 us; the launch traced here: 44.5 us
  starting transfers between devices  26 us (58%)
  Pallas kernels  9.93 us (22%)
  waiting for transfers between devices  4.45 us (10%)
  local copies, waits for them, and re-layouts  3.37 us (7%)
  other arithmetic  0.71 us (2%)
    ppermute x1, starting transfers between devices, shards(): lax.ppermute(source, 'layer', [((i + 1) % layers, i) for i in range(layer...  11.1 us
    all_to_all x1, starting transfers between devices, shards(): lax.all_to_all(chosen(place, staged(source), above), ('block', 'freq'), 0...  8.94 us
    all_to_all x1, starting transfers between devices, shards(): own = lax.all_to_all(repeated, 'freq', 0, 0)  5.96 us
    pallas_call x1, Pallas kernels, correlations_of(): pl.pallas_call(correlate, out_shape=jax.ShapeDtypeStruct((stations, SHIFT...  5.53 us
    all_to_all x1, waiting for transfers between devices, shards(): lax.all_to_all(chosen(place, staged(source), above), ('block', 'freq'), 0...  3.67 us
    unnamed x6, local copies, waits for them, and re-layouts  3.29 us
    pallas_call x1, Pallas kernels, whitened_block(): pl.pallas_call(whiten, out_shape=[jax.ShapeDtypeStruct((stations, F), jnp...  1.82 us
    pallas_call x1, Pallas kernels, prepared(): pl.pallas_call(prepare, out_shape=[jax.ShapeDtypeStruct((bands,) + spectr...  1.81 us
  transfers between devices with their start and end apart: 3, of which 2 were waited for; matrix products, arithmetic and copies ran while one was open for 2% of the time, Pallas kernels for 4%

profile of v3, /device:TPU:1, one launch (start us, length us, event | category | flops | bytes accessed | tf_op | source)
XLA Modules:
  0.0 44.5 jit_solution(17172146783148457935)
XLA Ops:
  0.0 1.8 %shard_map.55 = (bf16[8,2,64,256]{3,2,1,0:T(8,128)(2,1)}, bf16[8,16,256]{2,1,0:T(8,128)(2,1)}) custom-call(bf16[2,64,256]{2,1,0:T(8,128)(2,1)} %spectra_hbm.1, s32[1,64]{1,0:T(1,128)} %bitcast.4), custom_call_target="tpu_custom_call" | custom-call | flops 32768 | bytes 655360 | tf_op jit(solution)/shard_map/pallas_call | solution.py:87
  1.8 6.0 %all-to-all-start = ((bf16[8,2,64,256]{3,2,1,0:T(8,128)(2,1)}), bf16[8,2,64,256]{3,2,1,0:T(8,128)(2,1)S(1)}, u32[]{:S(2)}, u32[]{:S(2)}) async-start(bf16[8,2,64,256]{3,2,1,0:T(8,128)(2,1)} %get-tuple-element.14), calls=%async_computation | async-start | bytes 1048576 | tf_op jit(solution)/shard_map/all_to_all | solution.py:311
  7.8 11.1 %collective-permute-start = (bf16[8,16,256]{2,1,0:T(8,128)(2,1)}, bf16[8,16,256]{2,1,0:T(8,128)(2,1)S(1)}, u32[]{:S(2)}, u32[]{:S(2)}) collective-permute-start(bf16[8,16,256]{2,1,0:T(8,128)(2,1)} %get-tuple-element.13.source_ref), channel_id=1, source_target_pairs={{32,0},{64,32},{96,64},{128,96},{160,128},{192,160},{224,192},{256... | collective-permute-start | bytes 196616 | tf_op jit(solution)/shard_map/ppermute | solution.py:312
  18.9 0.0 copy-start.2
  18.9 0.8 %copy-done.2 = bf16[8,16,256]{2,1,0:T(8,128)(2,1)S(1)} copy-done((bf16[8,16,256]{2,1,0:T(8,128)(2,1)S(1)}, bf16[8,16,256]{2,1,0:T(8,128)(2,1)}, u32[]{:S(2)}) %copy-start.2) | copy-done | bytes 65560
  19.8 0.8 %collective-permute-done.above_ref = bf16[8,16,256]{2,1,0:T(8,128)(2,1)S(1)} collective-permute-done((bf16[8,16,256]{2,1,0:T(8,128)(2,1)}, bf16[8,16,256]{2,1,0:T(8,128)(2,1)S(1)}, u32[]{:S(2)}, u32[]{:S(2)}) %collective-permute-start) | collective-permute-done | bytes 65568 | tf_op jit(solution)/shard_map/ppermute | solution.py:312
  20.5 0.0 all-to-all-done.own_ref
  20.5 0.8 %shard_map.58 = bf16[32,16,256]{2,1,0:T(8,128)(2,1)} custom-call(s32[1]{0:T(128)} %bitcast.place_ref, bf16[8,16,256]{2,1,0:T(8,128)(2,1)S(1)} %shard_map.57.source_ref, bf16[8,16,256]{2,1,0:T(8,128)(2,1)S(1)} %collective-permute-done.above_ref), custom_call_target="tpu_custom_call" | custom-call | bytes 393216 | tf_op jit(solution)/shard_map/pallas_call | solution.py:145
  21.3 8.9 %all-to-all-start.1 = ((bf16[32,16,256]{2,1,0:T(8,128)(2,1)}), bf16[32,16,256]{2,1,0:T(8,128)(2,1)S(1)}, u32[]{:S(2)}, u32[]{:S(2)}) async-start(bf16[32,16,256]{2,1,0:T(8,128)(2,1)} %shard_map.58), calls=%async_computation.1 | async-start | bytes 524288 | tf_op jit(solution)/shard_map/all_to_all | solution.py:315
  30.2 0.7 %multiply_bitcast_fusion = f32[64,24]{0,1:T(8,128)S(1)} fusion(s32[64,3,8]{0,2,1:T(8,128)} %param.7), kind=kLoop, calls=%fused_computation | loop fusion | flops 3072 | bytes 12288 | tf_op jit(solution)/shard_map/mul | solution.py:316
  30.9 0.1 copy.7.mask_ref
  31.0 0.0 copy-start
  31.0 1.2 %copy-done = bf16[2048,256]{1,0:T(8,128)(2,1)S(1)} copy-done((bf16[2048,256]{1,0:T(8,128)(2,1)S(1)}, bf16[2048,256]{1,0:T(8,128)(2,1)}, u32[]{:S(2)}) %copy-start) | copy-done | bytes 1048600
  32.3 0.0 copy-start.1
  32.3 1.2 %copy-done.1 = bf16[2048,256]{1,0:T(8,128)(2,1)S(1)} copy-done((bf16[2048,256]{1,0:T(8,128)(2,1)S(1)}, bf16[2048,256]{1,0:T(8,128)(2,1)}, u32[]{:S(2)}) %copy-start.1) | copy-done | bytes 1048600
  33.5 1.8 %shard_map.56 = (bf16[64,2048]{1,0:T(8,128)(2,1)S(1)}, bf16[64,2048]{1,0:T(8,128)(2,1)S(1)}, bf16[2048,256]{1,0:T(8,128)(2,1)S(1)}, bf16[2048,256]{1,0:T(8,128)(2,1)S(1)}) custom-call(bf16[8,2,64,256]{3,2,1,0:T(8,128)(2,1)S(1)} %all-to-all-done.own_ref, bf16[2048,256]{1,0:T(8,128)(2,1)S(1)} %copy-done.1, bf16[2048,256]{1,0:T(8,128)(2,1)S(1)} %copy-done), custom_call_target="tpu_custom_call" | custom-call | flops 3932160 | bytes 1048576 | tf_op jit(solution)/shard_map/pallas_call | solution.py:180
  35.3 3.7 %all-to-all-done.1.part_ref = bf16[32,16,256]{2,1,0:T(8,128)(2,1)S(1)} async-done(((bf16[32,16,256]{2,1,0:T(8,128)(2,1)}), bf16[32,16,256]{2,1,0:T(8,128)(2,1)S(1)}, u32[]{:S(2)}, u32[]{:S(2)}) %all-to-all-start.1) | async-done | bytes 262176 | tf_op jit(solution)/shard_map/all_to_all | solution.py:315
  39.0 5.5 %shard_map.59 = f32[64,3,8,512]{3,2,1,0:T(8,128)} custom-call(s32[1]{0:T(128)} %bitcast.place_ref, bf16[64,2048]{1,0:T(8,128)(2,1)S(1)} %get-tuple-element.16.own_real, bf16[64,2048]{1,0:T(8,128)(2,1)S(1)} %get-tuple-element.17.own_imag, bf16[2048,256]{1,0:T(8,128)(2,1)S(1)} %get-tuple-element.18.cos_ref, bf16[2048,256]{1,0:T(8,128)(2,1)S(1)} %get-tuple-element.19.sin_ref, ...), custom_call_target="tpu_custom_call" | custom-call | flops 3221225472 | bytes 3145728 | tf_op jit(solution)/shard_map/pallas_call | solution.py:287
  (1 shorter events, 0.0 us)
Async XLA Ops:
  1.8 18.7 %all-to-all-start = ((bf16[8,2,64,256]{3,2,1,0:T(8,128)(2,1)}), bf16[8,2,64,256]{3,2,1,0:T(8,128)(2,1)S(1)}, u32[]{:S(2)}, u32[]{:S(2)}) async-start(bf16[8,2,64,256]{3,2,1,0:T(8,128)(2,1)} %get-tuple-element.14), calls=%async_computation | async-start | bytes 1048576 | tf_op jit(solution)/shard_map/all_to_all | solution.py:311
  7.8 12.7 %collective-permute-start = (bf16[8,16,256]{2,1,0:T(8,128)(2,1)}, bf16[8,16,256]{2,1,0:T(8,128)(2,1)S(1)}, u32[]{:S(2)}, u32[]{:S(2)}) collective-permute-start(bf16[8,16,256]{2,1,0:T(8,128)(2,1)} %get-tuple-element.13.source_ref), channel_id=1, source_target_pairs={{32,0},{64,32},{96,64},{128,96},{160,128},{192,160},{224,192},{256... | collective-permute-start | bytes 196616 | tf_op jit(solution)/shard_map/ppermute | solution.py:312
  18.9 0.8 %copy-start.2 = (bf16[8,16,256]{2,1,0:T(8,128)(2,1)S(1)}, bf16[8,16,256]{2,1,0:T(8,128)(2,1)}, u32[]{:S(2)}) copy-start(bf16[8,16,256]{2,1,0:T(8,128)(2,1)} %get-tuple-element.13.source_ref) | copy-start | bytes 196612
  21.3 17.7 %all-to-all-start.1 = ((bf16[32,16,256]{2,1,0:T(8,128)(2,1)}), bf16[32,16,256]{2,1,0:T(8,128)(2,1)S(1)}, u32[]{:S(2)}, u32[]{:S(2)}) async-start(bf16[32,16,256]{2,1,0:T(8,128)(2,1)} %shard_map.58), calls=%async_computation.1 | async-start | bytes 524288 | tf_op jit(solution)/shard_map/all_to_all | solution.py:315
  31.0 1.2 %copy-start = (bf16[2048,256]{1,0:T(8,128)(2,1)S(1)}, bf16[2048,256]{1,0:T(8,128)(2,1)}, u32[]{:S(2)}) copy-start(bf16[2048,256]{1,0:T(8,128)(2,1)} %constant.12.clone.sin_from) | copy-start | bytes 3145732
  32.3 1.2 %copy-start.1 = (bf16[2048,256]{1,0:T(8,128)(2,1)S(1)}, bf16[2048,256]{1,0:T(8,128)(2,1)}, u32[]{:S(2)}) copy-start(bf16[2048,256]{1,0:T(8,128)(2,1)} %constant.11.clone.cos_from) | copy-start | bytes 3145732

commit v4 on v3

--- a/solution.py
+++ b/solution.py
@@ -126,18 +126,17 @@
     )(source)
 
 
-def choose(place_ref, source_ref, above_ref, sent_ref):
+def choose(place_ref, source_ref, above_ref, sent_ref, sems):
     bands = source_ref.shape[0]
+
+    def copy(other, ref):
+        return pltpu.make_async_copy(ref, sent_ref.at[pl.ds(other * bands, bands)], sems.at[other])
+
     for other in range(LAYER):
-        to = sent_ref.at[other * bands:(other + 1) * bands]
-
-        @pl.when(other < place_ref[0])
-        def _():
-            to[...] = source_ref[...]
-
-        @pl.when(other >= place_ref[0])
-        def _():
-            to[...] = above_ref[...]
+        pl.when(other < place_ref[0])(lambda: copy(other, source_ref).start())
+        pl.when(other >= place_ref[0])(lambda: copy(other, above_ref).start())
+    for other in range(LAYER):
+        copy(other, source_ref).wait()
 
 
 def chosen(place, source, above):
@@ -146,7 +145,8 @@
         choose,
         out_shape=jax.ShapeDtypeStruct((LAYER * source.shape[0],) + source.shape[1:], source.dtype),
         in_specs=[pl.BlockSpec(memory_space=pltpu.SMEM)] + [vmem] * 2,
-        out_specs=vmem,
+        out_specs=pl.BlockSpec(memory_space=pl.ANY),
+        scratch_shapes=[pltpu.SemaphoreType.DMA((LAYER,))],
         compiler_params=pltpu.CompilerParams(vmem_limit_bytes=8 * MIB),
         cost_estimate=pl.CostEstimate(flops=0, bytes_accessed=2 * 6 * source.size, transcendentals=0),
     )(place, source, above)
@@ -264,11 +264,11 @@
     form(0)
     before = None
     for n in range(len(steps)):
-        pair = product(n)
         if n + 1 < len(steps):
             if steps[n + 1][0] == len(edges):
                 edges.append(whiten_part(len(edges)))
             form(n + 1)
+        pair = product(n)
         if before is not None:
             finish(n - 1, before, edges[steps[n - 1][0]])
             send(n - 1)

time: 45 us -> 45 us (level)
  no operation moved by 1% of the time
where the time goes in v4:
time: 45 us; the launch traced here: 44.5 us
  starting transfers between devices  26 us (58%)
  Pallas kernels  9.94 us (22%)
  waiting for transfers between devices  4.45 us (10%)
  local copies, waits for them, and re-layouts  3.37 us (7%)
  other arithmetic  0.71 us (2%)
    ppermute x1, starting transfers between devices, shards(): lax.ppermute(source, 'layer', [((i + 1) % layers, i) for i in range(layer...  11.1 us
    all_to_all x1, starting transfers between devices, shards(): lax.all_to_all(chosen(place, staged(source), above), ('block', 'freq'), 0...  8.95 us
    all_to_all x1, starting transfers between devices, shards(): own = lax.all_to_all(repeated, 'freq', 0, 0)  5.96 us
    pallas_call x1, Pallas kernels, correlations_of(): pl.pallas_call(correlate, out_shape=jax.ShapeDtypeStruct((stations, SHIFT...  5.57 us
    all_to_all x1, waiting for transfers between devices, shards(): lax.all_to_all(chosen(place, staged(source), above), ('block', 'freq'), 0...  3.67 us
    unnamed x6, local copies, waits for them, and re-layouts  3.29 us
    pallas_call x1, Pallas kernels, whitened_block(): pl.pallas_call(whiten, out_shape=[jax.ShapeDtypeStruct((stations, F), jnp...  1.82 us
    pallas_call x1, Pallas kernels, prepared(): pl.pallas_call(prepare, out_shape=[jax.ShapeDtypeStruct((bands,) + spectr...  1.81 us
  transfers between devices with their start and end apart: 3, of which 2 were waited for; matrix products, arithmetic and copies ran while one was open for 2% of the time, Pallas kernels for 4%

profile of v4, /device:TPU:1, one launch (start us, length us, event | category | flops | bytes accessed | tf_op | source)
XLA Modules:
  0.0 44.5 jit_solution(13042593120611591749)
XLA Ops:
  0.0 1.8 %shard_map.55 = (bf16[8,2,64,256]{3,2,1,0:T(8,128)(2,1)}, bf16[8,16,256]{2,1,0:T(8,128)(2,1)}) custom-call(bf16[2,64,256]{2,1,0:T(8,128)(2,1)} %spectra_hbm.1, s32[1,64]{1,0:T(1,128)} %bitcast.4), custom_call_target="tpu_custom_call" | custom-call | flops 32768 | bytes 655360 | tf_op jit(solution)/shard_map/pallas_call | solution.py:87
  1.8 6.0 %all-to-all-start = ((bf16[8,2,64,256]{3,2,1,0:T(8,128)(2,1)}), bf16[8,2,64,256]{3,2,1,0:T(8,128)(2,1)S(1)}, u32[]{:S(2)}, u32[]{:S(2)}) async-start(bf16[8,2,64,256]{3,2,1,0:T(8,128)(2,1)} %get-tuple-element.14), calls=%async_computation | async-start | bytes 1048576 | tf_op jit(solution)/shard_map/all_to_all | solution.py:311
  7.8 11.1 %collective-permute-start = (bf16[8,16,256]{2,1,0:T(8,128)(2,1)}, bf16[8,16,256]{2,1,0:T(8,128)(2,1)S(1)}, u32[]{:S(2)}, u32[]{:S(2)}) collective-permute-start(bf16[8,16,256]{2,1,0:T(8,128)(2,1)} %get-tuple-element.13.source_ref), channel_id=1, source_target_pairs={{32,0},{64,32},{96,64},{128,96},{160,128},{192,160},{224,192},{256... | collective-permute-start | bytes 196616 | tf_op jit(solution)/shard_map/ppermute | solution.py:312
  18.9 0.0 copy-start.2
  18.9 0.8 %copy-done.2 = bf16[8,16,256]{2,1,0:T(8,128)(2,1)S(1)} copy-done((bf16[8,16,256]{2,1,0:T(8,128)(2,1)S(1)}, bf16[8,16,256]{2,1,0:T(8,128)(2,1)}, u32[]{:S(2)}) %copy-start.2) | copy-done | bytes 65560
  19.8 0.8 %collective-permute-done.above_ref = bf16[8,16,256]{2,1,0:T(8,128)(2,1)S(1)} collective-permute-done((bf16[8,16,256]{2,1,0:T(8,128)(2,1)}, bf16[8,16,256]{2,1,0:T(8,128)(2,1)S(1)}, u32[]{:S(2)}, u32[]{:S(2)}) %collective-permute-start) | collective-permute-done | bytes 65568 | tf_op jit(solution)/shard_map/ppermute | solution.py:312
  20.5 0.0 all-to-all-done.own_ref
  20.5 0.7 %shard_map.58 = bf16[32,16,256]{2,1,0:T(8,128)(2,1)} custom-call(s32[1]{0:T(128)} %bitcast.place_ref, bf16[8,16,256]{2,1,0:T(8,128)(2,1)S(1)} %shard_map.57.source_ref, bf16[8,16,256]{2,1,0:T(8,128)(2,1)S(1)} %collective-permute-done.above_ref), custom_call_target="tpu_custom_call" | custom-call | bytes 393216 | tf_op jit(solution)/shard_map/pallas_call | solution.py:144
  21.3 8.9 %all-to-all-start.1 = ((bf16[32,16,256]{2,1,0:T(8,128)(2,1)}), bf16[32,16,256]{2,1,0:T(8,128)(2,1)S(1)}, u32[]{:S(2)}, u32[]{:S(2)}) async-start(bf16[32,16,256]{2,1,0:T(8,128)(2,1)} %shard_map.58), calls=%async_computation.1 | async-start | bytes 524288 | tf_op jit(solution)/shard_map/all_to_all | solution.py:315
  30.2 0.7 %multiply_bitcast_fusion = f32[64,24]{0,1:T(8,128)S(1)} fusion(s32[64,3,8]{0,2,1:T(8,128)} %param.7), kind=kLoop, calls=%fused_computation | loop fusion | flops 3072 | bytes 12288 | tf_op jit(solution)/shard_map/mul | solution.py:316
  30.9 0.1 copy.7.mask_ref
  31.0 0.0 copy-start
  31.0 1.2 %copy-done = bf16[2048,256]{1,0:T(8,128)(2,1)S(1)} copy-done((bf16[2048,256]{1,0:T(8,128)(2,1)S(1)}, bf16[2048,256]{1,0:T(8,128)(2,1)}, u32[]{:S(2)}) %copy-start) | copy-done | bytes 1048600
  32.2 0.0 copy-start.1
  32.2 1.2 %copy-done.1 = bf16[2048,256]{1,0:T(8,128)(2,1)S(1)} copy-done((bf16[2048,256]{1,0:T(8,128)(2,1)S(1)}, bf16[2048,256]{1,0:T(8,128)(2,1)}, u32[]{:S(2)}) %copy-start.1) | copy-done | bytes 1048600
  33.5 1.8 %shard_map.56 = (bf16[64,2048]{1,0:T(8,128)(2,1)S(1)}, bf16[64,2048]{1,0:T(8,128)(2,1)S(1)}, bf16[2048,256]{1,0:T(8,128)(2,1)S(1)}, bf16[2048,256]{1,0:T(8,128)(2,1)S(1)}) custom-call(bf16[8,2,64,256]{3,2,1,0:T(8,128)(2,1)S(1)} %all-to-all-done.own_ref, bf16[2048,256]{1,0:T(8,128)(2,1)S(1)} %copy-done.1, bf16[2048,256]{1,0:T(8,128)(2,1)S(1)} %copy-done), custom_call_target="tpu_custom_call" | custom-call | flops 3932160 | bytes 1048576 | tf_op jit(solution)/shard_map/pallas_call | solution.py:180
  35.3 3.7 %all-to-all-done.1.part_ref = bf16[32,16,256]{2,1,0:T(8,128)(2,1)S(1)} async-done(((bf16[32,16,256]{2,1,0:T(8,128)(2,1)}), bf16[32,16,256]{2,1,0:T(8,128)(2,1)S(1)}, u32[]{:S(2)}, u32[]{:S(2)}) %all-to-all-start.1) | async-done | bytes 262176 | tf_op jit(solution)/shard_map/all_to_all | solution.py:315
  39.0 5.6 %shard_map.59 = f32[64,3,8,512]{3,2,1,0:T(8,128)} custom-call(s32[1]{0:T(128)} %bitcast.place_ref, bf16[64,2048]{1,0:T(8,128)(2,1)S(1)} %get-tuple-element.16.own_real, bf16[64,2048]{1,0:T(8,128)(2,1)S(1)} %get-tuple-element.17.own_imag, bf16[2048,256]{1,0:T(8,128)(2,1)S(1)} %get-tuple-element.18.cos_ref, bf16[2048,256]{1,0:T(8,128)(2,1)S(1)} %get-tuple-element.19.sin_ref, ...), custom_call_target="tpu_custom_call" | custom-call | flops 3221225472 | bytes 3145728 | tf_op jit(solution)/shard_map/pallas_call | solution.py:287
  (1 shorter events, 0.0 us)
Async XLA Ops:
  1.8 18.7 %all-to-all-start = ((bf16[8,2,64,256]{3,2,1,0:T(8,128)(2,1)}), bf16[8,2,64,256]{3,2,1,0:T(8,128)(2,1)S(1)}, u32[]{:S(2)}, u32[]{:S(2)}) async-start(bf16[8,2,64,256]{3,2,1,0:T(8,128)(2,1)} %get-tuple-element.14), calls=%async_computation | async-start | bytes 1048576 | tf_op jit(solution)/shard_map/all_to_all | solution.py:311
  7.8 12.7 %collective-permute-start = (bf16[8,16,256]{2,1,0:T(8,128)(2,1)}, bf16[8,16,256]{2,1,0:T(8,128)(2,1)S(1)}, u32[]{:S(2)}, u32[]{:S(2)}) collective-permute-start(bf16[8,16,256]{2,1,0:T(8,128)(2,1)} %get-tuple-element.13.source_ref), channel_id=1, source_target_pairs={{32,0},{64,32},{96,64},{128,96},{160,128},{192,160},{224,192},{256... | collective-permute-start | bytes 196616 | tf_op jit(solution)/shard_map/ppermute | solution.py:312
  18.9 0.8 %copy-start.2 = (bf16[8,16,256]{2,1,0:T(8,128)(2,1)S(1)}, bf16[8,16,256]{2,1,0:T(8,128)(2,1)}, u32[]{:S(2)}) copy-start(bf16[8,16,256]{2,1,0:T(8,128)(2,1)} %get-tuple-element.13.source_ref) | copy-start | bytes 196612
  21.3 17.7 %all-to-all-start.1 = ((bf16[32,16,256]{2,1,0:T(8,128)(2,1)}), bf16[32,16,256]{2,1,0:T(8,128)(2,1)S(1)}, u32[]{:S(2)}, u32[]{:S(2)}) async-start(bf16[32,16,256]{2,1,0:T(8,128)(2,1)} %shard_map.58), calls=%async_computation.1 | async-start | bytes 524288 | tf_op jit(solution)/shard_map/all_to_all | solution.py:315
  31.0 1.2 %copy-start = (bf16[2048,256]{1,0:T(8,128)(2,1)S(1)}, bf16[2048,256]{1,0:T(8,128)(2,1)}, u32[]{:S(2)}) copy-start(bf16[2048,256]{1,0:T(8,128)(2,1)} %constant.12.clone.sin_from) | copy-start | bytes 3145732
  32.2 1.2 %copy-start.1 = (bf16[2048,256]{1,0:T(8,128)(2,1)S(1)}, bf16[2048,256]{1,0:T(8,128)(2,1)}, u32[]{:S(2)}) copy-start(bf16[2048,256]{1,0:T(8,128)(2,1)} %constant.11.clone.cos_from) | copy-start | bytes 3145732
